TPU v7x, 32 devices: a whole 2x2x4 slice. The times are simulated.
32 devices in a mesh: blk: 8 (over z, x), head: 4 (over y, core).
Axes of the slice: x: 2, y: 2, z: 4, core: 2. Of those that a mesh axis runs over, the one named last changes fastest.
Arguments:
- states_in: bfloat16 [2048, 2048], P('blk'), may hold values from -12 to 12
- w_qkv: bfloat16 [3, 2048, 2048], P(None, None, 'head'), may hold values from -0.35355339 to 0.35355339
- qk_gain: float32 [2, 2048], P(None, 'head'), may hold values from 0.8 to 7.8
- w_out: bfloat16 [2048, 2048], P('head'), may hold values from -0.125 to 0.125
- post_gain: float32 [2, 2048], replicated, may hold values from 0.5 to 1.5
- w_gate_up: bfloat16 [2, 2048, 8192], P(None, None, 'blk'), may hold values from -0.125 to 0.125
- w_down: bfloat16 [8192, 2048], P('blk'), may hold values from -0.0625 to 0.0625
- cache_keys: bfloat16 [8, 256, 2048], P('blk', None, 'head'), may hold values from -6 to 6
- cache_values: bfloat16 [8, 256, 2048], P('blk', None, 'head'), may hold values from -6 to 6
- slot_node: int32 [8], replicated, may hold values from 0 to 7, each once
- node_length: int32 [8], replicated, may hold values from 1 to 256, 1280 in all
- node_parent: int32 [4], replicated, may hold values from 0 to 3
- leaf_segment: int32 [8, 256], replicated, may hold values from 0 to 7, never falling along the last dimension, each value on 1 to 128 neighbouring positions
- leaf_node: int32 [8, 8], replicated, may hold values from 4 to 7
Outputs:
- layer_out: bfloat16 [2048, 2048], P(('blk', 'head'))
Inputs may be any that keep to these rules, and one draw needn't show every extreme that they name: Slot s holds node slot_node[s]; every node is held once. Rows 0 to node_length[n] - 1 of node n's slot are valid; the longest node has 256 rows. Nodes 0 to 3 are roots; middle node 4 + i hangs under root node_parent[i]. `leaf_segment`: never falls along a group; every leaf of a group has 1 to 128 tokens. `leaf_node`: every leaf hangs under a middle node.
All inputs are finite; a program needn't handle non-finite values.
Results may differ from a plain program's by a relative error of at most 0.025.
Values may be sent and summed in bfloat16 or wider, within the bound.
A program may use at most 192 MiB of HBM per device.

v0:
```python
import jax
import jax.numpy as jnp
from jax import lax
from jax.sharding import PartitionSpec as P

HD = 128


EPS = 1e-06
THETA = 500000.0
NEG = -1e30


def tree_info(leaf_segment, leaf_node, node_parent, node_length):
    groups, tok_rows = leaf_segment.shape
    leaf_count = leaf_node.shape[1]
    middles = node_parent.shape[0]
    all_nodes = node_length.shape[0]
    tenant_count = all_nodes - middles
    leaf_ids = jnp.arange(leaf_count, dtype=jnp.int32)
    onehot = (leaf_segment[:, :, None] == leaf_ids[None, None, :]).astype(jnp.int32)
    middle = jnp.sum(onehot * leaf_node[:, None, :], axis=-1)
    counts = jnp.sum(onehot, axis=1)
    starts = jnp.cumsum(counts, axis=1) - counts
    first_at = jnp.sum(onehot * starts[:, None, :], axis=-1)
    middle_ids = jnp.arange(middles, dtype=jnp.int32) + tenant_count
    root_node = jnp.sum(jnp.where(middle[..., None] == middle_ids, node_parent, 0), axis=-1)
    node_ids = jnp.arange(all_nodes, dtype=jnp.int32)
    len_middle = jnp.sum(jnp.where(middle[..., None] == node_ids, node_length, 0), axis=-1)
    len_root = jnp.sum(jnp.where(root_node[..., None] == node_ids, node_length, 0), axis=-1)
    offsets = jnp.arange(tok_rows, dtype=jnp.int32)[None, :] - first_at
    position = len_root + len_middle + offsets
    return (middle, root_node, position)


def rotate(values_in, position):
    half_size = values_in.shape[-1] // 2
    frequency = THETA ** (-2.0 * jnp.arange(half_size, dtype=jnp.float32) / values_in.shape[-1])
    angles = position.astype(jnp.float32)[:, None] * frequency[None, :]
    cosine = jnp.cos(angles)[:, None, :]
    sine_part = jnp.sin(angles)[:, None, :]
    lower = values_in[..., :half_size]
    upper = values_in[..., half_size:]
    return jnp.concatenate(
        [lower * cosine - upper * sine_part, upper * cosine + lower * sine_part], axis=-1
    )


def rms_norm(values_in, gain):
    return (
        values_in * lax.rsqrt(jnp.mean(values_in * values_in, axis=-1, keepdims=True) + EPS) * gain
    )


def lookup_length(nodes, node_length):
    node_ids = jnp.arange(node_length.shape[0], dtype=jnp.int32)
    return jnp.sum(jnp.where(nodes[:, None] == node_ids[None, :], node_length[None, :], 0), axis=-1)


def masked_partial(scores, visible, values_in):
    masked = jnp.where(visible, scores, NEG)
    peak = jnp.max(masked, axis=-1)
    weights = jnp.where(visible, jnp.exp(masked - peak[..., None]), 0.0)
    totals = jnp.sum(weights, axis=-1)
    summed = jnp.einsum(
        "rhk,khe->rhe", weights.astype(jnp.bfloat16), values_in, preferred_element_type=jnp.float32
    )
    return (peak, totals, summed)


def combine(left, right):
    peak = jnp.maximum(left[0], right[0])
    scale_left = jnp.exp(left[0] - peak)
    scale_right = jnp.exp(right[0] - peak)
    totals = left[1] * scale_left + right[1] * scale_right
    summed = left[2] * scale_left[..., None] + right[2] * scale_right[..., None]
    return (peak, totals, summed)


def cache_partial(queries, middle, root_node, keys_in, values_in, nodes, lengths):
    slots, node_rows, columns = keys_in.shape
    head_count, size = (queries.shape[1], queries.shape[2])
    flat_keys = keys_in.reshape(slots * node_rows, head_count, size)
    flat_values = values_in.reshape(slots * node_rows, head_count, size)
    node_flat = jnp.broadcast_to(nodes[:, None], (slots, node_rows)).reshape(-1)
    length_flat = jnp.broadcast_to(lengths[:, None], (slots, node_rows)).reshape(-1)
    row_flat = jnp.broadcast_to(
        jnp.arange(node_rows, dtype=jnp.int32)[None, :], (slots, node_rows)
    ).reshape(-1)
    visible = (
        (node_flat[None, :] == middle[:, None]) | (node_flat[None, :] == root_node[:, None])
    ) & (row_flat < length_flat)[None, :]
    scores = jnp.einsum(
        "rhe,khe->rhk", queries, flat_keys, preferred_element_type=jnp.float32
    ) * size ** (-0.5)
    return masked_partial(scores, visible[:, None, :], flat_values)


def on_device(
    states_in,
    w_qkv,
    qk_gain,
    w_out,
    post_gain,
    w_gate_up,
    w_down,
    cache_keys,
    cache_values,
    slot_node,
    node_length,
    node_parent,
    leaf_segment,
    leaf_node,
):
    blk_index = lax.axis_index("blk")
    head_index = lax.axis_index("head")
    head_devices = lax.axis_size("head")
    tok_rows = states_in.shape[0]
    heads_here = w_qkv.shape[2] // HD
    columns = w_qkv.shape[2] * head_devices
    qkv_raw = jnp.einsum("td,cdw->ctw", states_in, w_qkv, preferred_element_type=jnp.float32)
    query_squares, key_squares = lax.psum(
        (jnp.sum(qkv_raw[0] * qkv_raw[0], axis=1), jnp.sum(qkv_raw[1] * qkv_raw[1], axis=1)), "head"
    )
    middle_all, root_all, position_all = tree_info(
        leaf_segment, leaf_node, node_parent, node_length
    )
    position = lax.dynamic_index_in_dim(position_all, blk_index, 0, keepdims=False)
    middle_own = lax.dynamic_index_in_dim(middle_all, blk_index, 0, keepdims=False)
    root_own = lax.dynamic_index_in_dim(root_all, blk_index, 0, keepdims=False)
    segment_own = lax.dynamic_index_in_dim(leaf_segment, blk_index, 0, keepdims=False)

    def normed(raw_part, squares, gain):
        scaled = raw_part * lax.rsqrt(squares / columns + EPS)[:, None] * gain
        return rotate(scaled.reshape(tok_rows, heads_here, HD), position).astype(jnp.bfloat16)

    queries = normed(qkv_raw[0], query_squares, qk_gain[0])
    keys_new = normed(qkv_raw[1], key_squares, qk_gain[1])
    values_cast = qkv_raw[2].astype(jnp.bfloat16).reshape(tok_rows, heads_here, HD)
    order = jnp.arange(tok_rows, dtype=jnp.int32)
    see_leaf = (segment_own[:, None] == segment_own[None, :]) & (order[None, :] <= order[:, None])
    leaf_scores = jnp.einsum(
        "rhe,khe->rhk", queries, keys_new, preferred_element_type=jnp.float32
    ) * HD ** (-0.5)
    local_state = masked_partial(leaf_scores, see_leaf[:, None, :], values_cast)
    keys_piece = lax.all_gather(cache_keys, "blk", axis=0, tiled=True)
    values_piece = lax.all_gather(cache_values, "blk", axis=0, tiled=True)
    lengths = lookup_length(slot_node, node_length)
    needed = jnp.any(
        (slot_node[:, None] == middle_own[None, :]) | (slot_node[:, None] == root_own[None, :])
    )

    def attend(carry):
        return combine(
            carry,
            cache_partial(
                queries, middle_own, root_own, keys_piece, values_piece, slot_node, lengths
            ),
        )

    def keep(carry):
        return carry

    state = lax.cond(needed, attend, keep, local_state)
    attended = (
        (state[2] / state[1][..., None]).astype(jnp.bfloat16).reshape(tok_rows, heads_here * HD)
    )
    attn_part = jnp.dot(attended, w_out, preferred_element_type=jnp.float32)
    own_rows = tok_rows // head_devices
    attn_whole = lax.psum(attn_part.astype(jnp.bfloat16), "head").astype(jnp.float32)
    attn_proj = lax.dynamic_slice_in_dim(attn_whole, head_index * own_rows, own_rows, 0)
    state_rows = lax.dynamic_slice_in_dim(states_in, head_index * own_rows, own_rows, 0)
    mid_state = (state_rows.astype(jnp.float32) + rms_norm(attn_proj, post_gain[0])).astype(
        jnp.bfloat16
    )
    gate_up = jnp.einsum(
        "rd,cdf->crf",
        lax.all_gather(mid_state, "blk", axis=0, tiled=True),
        w_gate_up,
        preferred_element_type=jnp.float32,
    )
    hidden = (jax.nn.silu(gate_up[0]) * gate_up[1]).astype(jnp.bfloat16)
    mlp_proj = lax.psum_scatter(
        jnp.dot(hidden, w_down, preferred_element_type=jnp.float32).astype(jnp.bfloat16),
        "blk",
        scatter_dimension=0,
        tiled=True,
    ).astype(jnp.float32)
    return (mid_state.astype(jnp.float32) + rms_norm(mlp_proj, post_gain[1])).astype(jnp.bfloat16)


def solution(mesh):
    placed = (
        P("blk", None),
        P(None, None, "head"),
        P(None, "head"),
        P("head", None),
        P(),
        P(None, None, "blk"),
        P("blk", None),
        P("blk", None, "head"),
        P("blk", None, "head"),
        P(),
        P(),
        P(),
        P(),
        P(),
    )
    return jax.shard_map(
        on_device, mesh=mesh, in_specs=placed, out_specs=P(("blk", "head"), None), check_vma=False
    )
```

profile of v0, /device:TPU:0, one launch (start us, length us, event | category | flops | bytes accessed | tf_op | source)
XLA Modules:
  0.0 315.0 jit_solution(4344316091295949839)
XLA Ops:
  6.5 0.7 all-gather.4.cloned.1.call-update
  7.3 0.7 all-gather.6.cloned.1.call-update
  8.1 0.9 convert_reduce_fusion
  9.0 0.2 reduce_window_sum.11
  9.1 4.9 %convolution_bitcast_fusion.1 = f32[3,256,512]{1,2,0:T(8,128)S(1)} fusion(bf16[3,2048,512]{2,1,0:T(8,128)(2,1)} %param.17, bf16[256,2048]{1,0:T(8,128)(2,1)} %param.16), kind=kOutput, calls=%fused_computation.33 | convolution fusion | flops 1610612736 | bytes 8912896 | tf_op jit(solution)/shard_map/td,cdw->ctw/dot_general | solution.py:121
  14.2 0.7 slice.87
  14.9 0.1 multiply_reduce_fusion.1
  15.0 1.0 copy.49
  16.0 0.2 copy.48
  16.2 0.1 select_reduce_fusion.1
  16.4 0.1 select_reduce_fusion.5
  16.5 0.7 or_reduce_fusion
  17.8 8.5 %all-reduce = (f32[256]{0:T(256)S(1)}, f32[256]{0:T(256)S(1)}) all-reduce(f32[256]{0:T(256)S(1)} %get-tuple-element.109, f32[256]{0:T(256)S(1)} %get-tuple-element.108), channel_id=1, replica_groups=mesh['blk'=8,'head'=4] {'head'}, use_global_device_ids=true, to_apply=%region_11.12 | all-reduce | flops 512 | bytes 4096 | tf_op jit(solution)/shard_map/psum | solution.py:122
  26.3 0.1 select_reduce_fusion.3
  26.5 0.5 multiply_cosine_fusion
  27.0 1.2 multiply_multiply_fusion
  28.2 0.1 multiply_multiply_fusion.1
  28.3 0.4 subtract_convert_fusion.1
  28.8 0.1 pad_maximum_fusion
  28.9 0.1 fusion.54
  29.0 0.4 fusion.66
  29.4 0.2 fusion.38
  29.6 0.3 convolution_bitcast_fusion.2
  30.0 31.5 %all-gather.4.cloned.1.call-done = bf16[8,256,512]{2,1,0:T(8,128)(2,1)} async-done(((bf16[1,256,512]{2,1,0:T(8,128)(2,1)}), bf16[8,256,512]{2,1,0:T(8,128)(2,1)}) %all-gather.4.cloned.1.call-update) | async-done | bytes 2097168 | tf_op jit(solution)/shard_map/all_gather | solution.py:146
  61.5 49.9 %all-gather.6.cloned.1.call-done = bf16[8,256,512]{2,1,0:T(8,128)(2,1)} async-done(((bf16[1,256,512]{2,1,0:T(8,128)(2,1)}), bf16[8,256,512]{2,1,0:T(8,128)(2,1)}) %all-gather.6.cloned.1.call-update) | async-done | bytes 2097168 | tf_op jit(solution)/shard_map/all_gather | solution.py:147
  111.4 26.4 %conditional.1 = ((f32[256,4]{0,1:T(4,128)S(1)}, f32[256,4,128]{0,2,1:T(8,128)S(1)})) conditional(s32[]{:T(128)} %convert_element_type.61, (f32[256,4]{0,1:T(4,128)S(1)}, f32[256,4,128]{0,2,1:T(8,128)S(1)}) %tuple.12, (s32[8]{0:T(128)S(1)}, s32[256]{0:T(256)S(1)}, s32[256]{0:T(256)S(1)}, s32[8,8]{1,0:T(8,128)S(1)}, s32[8]{0:T(128)S(1)}, ...), branch_computations={%region_14.15_spmd, %region_15.19_spmd} | conditional | flops 1103501568 | bytes 76904920 | solution.py:164
  111.4 0.1 broadcast_bitcast_fusion
  111.5 0.2 select_reduce_fusion
  111.7 0.1 iota_compare_fusion
  111.8 1.5 or_and_fusion
  113.3 4.0 %reshape.255 = bf16[2048,4,128]{2,1,0:T(4,128)(2,1)} reshape(bf16[8,256,512]{2,1,0:T(8,128)(2,1)} %get-tuple-element.47) | data formatting | bytes 4194304 | tf_op jit(solution)/shard_map/cond/branch_1_fun/reshape | solution.py:83
  117.3 3.1 fusion
  120.4 2.1 fusion.2
  122.5 1.1 copy-done.1
  123.6 4.0 %reshape.256 = bf16[2048,4,128]{2,1,0:T(4,128)(2,1)} reshape(bf16[8,256,512]{2,1,0:T(8,128)(2,1)} %get-tuple-element.50) | data formatting | bytes 4194304 | tf_op jit(solution)/shard_map/cond/branch_1_fun/reshape | solution.py:84
  127.6 1.0 copy.52
  128.6 8.0 %fusion.19 = f32[256,4,128]{2,0,1:T(8,128)} fusion(bf16[2048,4,128]{2,1,0:T(4,128)(2,1)} %reshape.256, f32[4,2048,256]{2,1,0:T(8,128)} %copy-done.1, f32[256,4]{0,1:T(4,128)S(1)} %get-tuple-element.119, pred[256,2048]{0,1:T(8,128)(4,1)S(1)} %or_and_fusion, f32[256,4,128]{2,0,1:T(8,128)} %copy.52, f32[256,4]{0,1:T(4,128)S(1)} %get-tuple-element.118, ...), kind=kOutput, calls=%fused_computation.13 | convolution fusion | flops 547749888 | bytes 12070912 | tf_op jit(solution)/shard_map/cond/branch_1_fun/rhk,khe->rhe/dot_general | solution.py:65
  136.6 1.2 copy.58
  137.9 1.8 convolution_convert_fusion.1
  139.8 34.7 %all-reduce.3.cloned.1.call-done = bf16[256,2048]{1,0:T(8,128)(2,1)} async-done(((bf16[256,2048]{1,0:T(8,128)(2,1)}), bf16[256,2048]{1,0:T(8,128)(2,1)}) %all-reduce.3.cloned.1.call-update) | async-done | bytes 1048592 | tf_op jit(solution)/shard_map/psum | solution.py:170
  174.4 1.1 fusion.42
  175.6 1.9 fusion.41
  177.5 49.8 %all-gather.8.cloned.1.call-done = bf16[512,2048]{1,0:T(8,128)(2,1)} async-done(((bf16[64,2048]{1,0:T(8,128)(2,1)}), bf16[512,2048]{1,0:T(8,128)(2,1)}) %all-gather.8.cloned.1.call-update) | async-done | bytes 2097168 | tf_op jit(solution)/shard_map/all_gather | solution.py:178
  227.3 7.7 %convolution_bitcast_fusion = f32[2,512,1024]{2,1,0:T(8,128)S(1)} fusion(bf16[2,2048,1024]{2,1,0:T(8,128)(2,1)} %param.21, bf16[512,2048]{1,0:T(8,128)(2,1)} %all-gather.8.cloned.1.call-done), kind=kOutput, calls=%fused_computation.27 | convolution fusion | flops 4294967296 | bytes 14680064 | tf_op jit(solution)/shard_map/rd,cdf->crf/dot_general | solution.py:176
  235.0 3.7 %convolution_convert_fusion = bf16[512,2048]{1,0:T(8,128)(2,1)} fusion(bf16[1024,2048]{1,0:T(8,128)(2,1)S(1)} %copy-done.11, f32[2,512,1024]{2,1,0:T(8,128)S(1)} %convolution_bitcast_fusion), kind=kOutput, calls=%fused_computation.25 | convolution fusion | flops 2151677952 | bytes 10485760 | tf_op jit(solution)/shard_map/dot_general | solution.py:184
  238.8 66.7 %reduce-scatter.2.cloned.1.call-done = bf16[64,2048]{1,0:T(8,128)(2,1)} async-done(((bf16[512,2048]{1,0:T(8,128)(2,1)}), bf16[64,2048]{1,0:T(8,128)(2,1)}) %reduce-scatter.2.cloned.1.call-update) | async-done | bytes 262160 | tf_op jit(solution)/shard_map/reduce_scatter | solution.py:183
  305.5 1.1 fusion.43
  306.6 1.8 fusion.46
  (46 shorter events, 0.5 us)
Async XLA Ops:
  6.5 131.4 %copy-start = (bf16[512,2048]{1,0:T(8,128)(2,1)S(1)}, bf16[512,2048]{1,0:T(8,128)(2,1)}, u32[]{:S(2)}) copy-start(bf16[512,2048]{1,0:T(8,128)(2,1)} %param.19) | copy-start | bytes 6291460
  6.5 55.0 %all-gather.4.cloned.1.call-start = ((), (), s32[]{:S(2)}) async-start(), calls=%async_computation.1 | async-start | bytes 2359296 | tf_op jit(solution)/shard_map/all_gather | solution.py:146
  7.3 104.2 %all-gather.6.cloned.1.call-start = ((), (), s32[]{:S(2)}) async-start(), calls=%async_computation.2 | async-start | bytes 2359296 | tf_op jit(solution)/shard_map/all_gather | solution.py:147
  8.0 166.4 %all-reduce.3.cloned.1.call-start = ((), (), s32[]{:S(2)}) async-start(), calls=%async_computation.3 | async-start | bytes 2097152 | tf_op jit(solution)/shard_map/psum | solution.py:170
  14.1 2.1 copy-start.4
  14.1 2.1 copy-start.8
  14.1 2.3 copy-start.10
  14.1 2.3 copy-start.6
  14.1 12.2 %copy-start.9 = (s32[8]{0:T(128)S(1)}, s32[8]{0:T(128)}, u32[]{:S(2)}) copy-start(s32[8]{0:T(128)} %param.26) | copy-start | bytes 100
  14.1 12.3 %copy-start.7 = (f32[2,512]{1,0:T(2,128)S(1)}, f32[2,512]{1,0:T(2,128)}, u32[]{:S(2)}) copy-start(f32[2,512]{1,0:T(2,128)} %param.18) | copy-start | bytes 12292
  28.2 1.4 copy-start.3
  120.4 3.2 %copy-start.1 = (f32[4,2048,256]{2,1,0:T(8,128)}, f32[4,2048,256]{2,1,0:T(8,128)S(1)}, u32[]{:S(2)}) copy-start(f32[4,2048,256]{2,1,0:T(8,128)S(1)} %get-tuple-element.120) | copy-start | bytes 25165828 | tf_op jit(solution)/shard_map/cond
  137.8 1.9 copy-start.5
  139.7 87.6 %all-gather.8.cloned.1.call-start = ((), (), s32[]{:S(2)}) async-start(), calls=%async_computation.4 | async-start | bytes 2359296 | tf_op jit(solution)/shard_map/all_gather | solution.py:178
  177.5 128.0 %reduce-scatter.2.cloned.1.call-start = ((), (), s32[]{:S(2)}) async-start(), calls=%async_computation.5 | async-start | bytes 2359296 | tf_op jit(solution)/shard_map/reduce_scatter | solution.py:183
  227.3 7.7 %copy-start.11 = (bf16[1024,2048]{1,0:T(8,128)(2,1)S(1)}, bf16[1024,2048]{1,0:T(8,128)(2,1)}, u32[]{:S(2)}) copy-start(bf16[1024,2048]{1,0:T(8,128)(2,1)} %param.22) | copy-start | bytes 12582916
  235.0 71.6 %copy-start.2 = (bf16[64,2048]{1,0:T(8,128)(2,1)S(1)}, bf16[64,2048]{1,0:T(8,128)(2,1)}, u32[]{:S(2)}) copy-start(bf16[64,2048]{1,0:T(8,128)(2,1)} %fusion.41) | copy-start | bytes 786436
Sparse Core Ops, SparseCore 0:
  9.5 51.9 all-gather.3
  63.6 47.7 all-gather.5
  139.8 34.5 all-reduce.2
  177.6 49.6 all-gather.7
  238.9 66.5 reduce-scatter.1
where the time goes:
time: 316 us; the launch traced here: 315 us
  waiting for transfers between devices  234 us (74%)
  matrix products  29.9 us (9%)
  other arithmetic  14.8 us (5%)
  between operations  14.1 us (4%)
  local copies, waits for them, and re-layouts  13.4 us (4%)
  blocking collectives  8.5 us (3%)
    reduce_scatter x1, waiting for transfers between devices, on_device(): lax.psum_scatter(jnp.dot(hidden, w_down, preferred_element_type=jnp.float...  66.7 us
    all_gather x1, waiting for transfers between devices, on_device(): values_piece = lax.all_gather(cache_values, 'blk', axis=0, tiled=True)  49.9 us
    all_gather x1, waiting for transfers between devices, on_device(): lax.all_gather(mid_state, 'blk', axis=0, tiled=True)  49.8 us
    psum x1, waiting for transfers between devices, on_device(): lax.psum(attn_part.astype(jnp.bfloat16), 'head').astype(jnp.float32)  34.7 us
    all_gather x1, waiting for transfers between devices, on_device(): keys_piece = lax.all_gather(cache_keys, 'blk', axis=0, tiled=True)  31.5 us
    psum x1, blocking collectives, on_device(): lax.psum((jnp.sum(qkv_raw[0] * qkv_raw[0], axis=1), jnp.sum(qkv_raw[1] *...  8.5 us
    dot_general x2, matrix products, masked_partial(): jnp.einsum('rhk,khe->rhe', weights.astype(jnp.bfloat16), values_in, prefe...  8.31 us
    dot_general x1, matrix products, on_device(): jnp.einsum('rd,cdf->crf', lax.all_gather(mid_state, 'blk', axis=0, tiled=...  7.69 us
  transfers between devices with their start and end apart: 5, of which 5 were waited for; matrix products, arithmetic and copies ran while one was open for 4% of the time, Pallas kernels for 0%

commit v1 on v0

--- a/solution.py
+++ b/solution.py
@@ -1,14 +1,200 @@
+import functools
+
 import jax
 import jax.numpy as jnp
 from jax import lax
+from jax.experimental import pallas as pl
+from jax.experimental.pallas import tpu as pltpu
 from jax.sharding import PartitionSpec as P
 
 HD = 128
-
-
 EPS = 1e-06
 THETA = 500000.0
 NEG = -1e30
+MESH = pl.DeviceIdType.MESH
+BF16 = jnp.bfloat16
+F32 = jnp.float32
+
+
+def by_distance(at, count, step):
+    back = count - 1 - at
+    near = jnp.minimum(at, back)
+    both = jnp.where(step % 2 == 1, at - (step + 1) // 2, at + step // 2)
+    return jnp.where(step <= 2 * near, both, jnp.where(at < back, step, count - 1 - step))
+
+
+def remote(src, dst, send_sem, recv_sem, **where):
+    return pltpu.make_async_remote_copy(
+        src_ref=src,
+        dst_ref=dst,
+        send_sem=send_sem,
+        recv_sem=recv_sem,
+        device_id=where,
+        device_id_type=MESH,
+    )
+
+
+def meet(peers):
+    barrier = pltpu.get_barrier_semaphore()
+    for peer in peers:
+        pl.semaphore_signal(barrier, inc=1, device_id=peer, device_id_type=MESH)
+    pl.semaphore_wait(barrier, len(peers))
+
+
+def mlp_kernel(
+    lines,
+    mid_ref, wgu_hbm, wd_hbm, gain_ref, out_ref,
+    gathered, wgu, wd, hidden, whole, own_part, send_x, recv_x, send_z, recv_z,
+    w_sem, g_send, g_recv, x_send, x_recv, z_send, z_recv,
+):
+    rows, width = mid_ref.shape
+    units = wd.shape[0]
+    me = lax.axis_index("blk")
+    z, x = me // 2, me % 2
+    other = z * 2 + 1 - x
+
+    loads = [
+        pltpu.make_async_copy(wgu_hbm.at[0], wgu.at[0], w_sem.at[0]),
+        pltpu.make_async_copy(wgu_hbm.at[1], wgu.at[1], w_sem.at[1]),
+        pltpu.make_async_copy(wd_hbm, wd, w_sem.at[2]),
+    ]
+    for load in loads:
+        load.start()
+    meet([{"blk": other}] + [{"blk": (z + j) % lines * 2 + x} for j in range(1, lines)])
+
+    def block(index):
+        return gathered.at[pl.ds(pl.multiple_of(index * rows, rows), rows)]
+
+    def pass_on(index, way, target):
+        return remote(block(index), block(index), g_send.at[way, index], g_recv.at[index], blk=target)
+
+    def spread(origin, wait):
+        index = origin * 2 + x
+        if wait:
+            pass_on(index, 0, other).wait_recv()
+        pass_on(index, 0, other).start()
+
+        @pl.when((origin <= z) & (z < lines - 1))
+        def _():
+            pass_on(index, 1, me + 2).start()
+
+        @pl.when((origin >= z) & (z > 0))
+        def _():
+            pass_on(index, 2, me - 2).start()
+
+    gathered[pl.ds(pl.multiple_of(me * rows, rows), rows), :] = mid_ref[...]
+    spread(z, False)
+
+    def to_x(origin):
+        return remote(send_x.at[origin], recv_x.at[origin], x_send.at[origin], x_recv.at[origin], blk=other)
+
+    def to_z(origin):
+        return remote(send_z.at[origin], recv_z.at[z], z_send.at[origin], z_recv.at[z], blk=origin * 2 + x)
+
+    def reduce_x(origin):
+        to_x(origin).wait_recv()
+        summed = own_part[origin] + recv_x[origin].astype(F32)
+        own_part[origin] = summed
+        send_z[origin] = summed.astype(BF16)
+
+        @pl.when(origin != z)
+        def _():
+            to_z(origin).start()
+
+    tile = min(256, units)
+    wide = min(512, width)
+    for step in range(lines):
+        origin = by_distance(z, lines, step)
+        if step + 1 < lines:
+            spread(by_distance(z, lines, step + 1), True)
+        pass_on(origin * 2 + 1 - x, 0, other).wait_recv()
+        if step == 0:
+            loads[0].wait()
+            loads[1].wait()
+        chunk = pl.ds(pl.multiple_of(origin * 2 * rows, 2 * rows), 2 * rows)
+
+        @pl.loop(0, units // tile)
+        def _(t):
+            at = pl.ds(pl.multiple_of(t * tile, tile), tile)
+            state = gathered[chunk, :]
+            gate = jnp.dot(state, wgu[0, :, at], preferred_element_type=F32)
+            up = jnp.dot(state, wgu[1, :, at], preferred_element_type=F32)
+            hidden[:, at] = (gate / (1.0 + jnp.exp(-gate)) * up).astype(BF16)
+
+        if step == 0:
+            loads[2].wait()
+
+        @pl.loop(0, width // wide)
+        def _(t):
+            at = pl.ds(pl.multiple_of(t * wide, wide), wide)
+            whole[:, at] = jnp.dot(hidden[...], wd[:, at], preferred_element_type=F32)
+
+        own_part[origin] = whole[pl.ds(pl.multiple_of(x * rows, rows), rows), :]
+        send_x[origin] = whole[pl.ds(pl.multiple_of((1 - x) * rows, rows), rows), :].astype(BF16)
+        to_x(origin).start()
+        if step > 0:
+            reduce_x(by_distance(z, lines, step - 1))
+    reduce_x(by_distance(z, lines, lines - 1))
+
+    total = own_part[z]
+    for j in range(1, lines):
+        source = (z + j) % lines
+        remote(send_z.at[0], recv_z.at[source], z_send.at[0], z_recv.at[source], blk=other).wait_recv()
+        total = total + recv_z[source].astype(F32)
+    scale = lax.rsqrt(jnp.mean(total * total, axis=-1, keepdims=True) + EPS)
+    out_ref[...] = (mid_ref[...].astype(F32) + total * scale * gain_ref[...]).astype(BF16)
+
+    for origin in range(lines):
+        index = origin * 2 + x
+        to_x(origin).wait_send()
+        pass_on(index, 0, other).wait_send()
+
+        @pl.when((origin <= z) & (z < lines - 1))
+        def _():
+            pass_on(index, 1, me + 2).wait_send()
+
+        @pl.when((origin >= z) & (z > 0))
+        def _():
+            pass_on(index, 2, me - 2).wait_send()
+
+        @pl.when(origin != z)
+        def _():
+            to_z(origin).wait_send()
+
+
+def mlp(mid_state, w_gate_up, w_down, gain, devices):
+    rows, width = mid_state.shape
+    units = w_down.shape[0]
+    lines = devices // 2
+    vmem = pl.BlockSpec(memory_space=pltpu.VMEM)
+    hbm = pl.BlockSpec(memory_space=pl.ANY)
+    dma = pltpu.SemaphoreType.DMA
+    part = pltpu.VMEM((lines, rows, width), BF16)
+    return pl.pallas_call(
+        functools.partial(mlp_kernel, lines),
+        out_shape=jax.ShapeDtypeStruct((rows, width), BF16),
+        in_specs=[vmem, hbm, hbm, vmem],
+        out_specs=vmem,
+        scratch_shapes=[
+            pltpu.VMEM((devices * rows, width), BF16),
+            pltpu.VMEM(w_gate_up.shape, BF16),
+            pltpu.VMEM(w_down.shape, BF16),
+            pltpu.VMEM((2 * rows, units), BF16),
+            pltpu.VMEM((2 * rows, width), F32),
+            pltpu.VMEM((lines, rows, width), F32),
+            part, part, part, part,
+            dma((3,)),
+            dma((3, devices)),
+            dma((devices,)),
+            dma((lines,)),
+            dma((lines,)),
+            dma((lines,)),
+            dma((lines,)),
+        ],
+        compiler_params=pltpu.CompilerParams(
+            collective_id=1, has_side_effects=True, vmem_limit_bytes=60 * 2**20
+        ),
+    )(mid_state, w_gate_up, w_down, gain)
 
 
 def tree_info(leaf_segment, leaf_node, node_parent, node_length):
@@ -173,20 +359,7 @@
     mid_state = (state_rows.astype(jnp.float32) + rms_norm(attn_proj, post_gain[0])).astype(
         jnp.bfloat16
     )
-    gate_up = jnp.einsum(
-        "rd,cdf->crf",
-        lax.all_gather(mid_state, "blk", axis=0, tiled=True),
-        w_gate_up,
-        preferred_element_type=jnp.float32,
-    )
-    hidden = (jax.nn.silu(gate_up[0]) * gate_up[1]).astype(jnp.bfloat16)
-    mlp_proj = lax.psum_scatter(
-        jnp.dot(hidden, w_down, preferred_element_type=jnp.float32).astype(jnp.bfloat16),
-        "blk",
-        scatter_dimension=0,
-        tiled=True,
-    ).astype(jnp.float32)
-    return (mid_state.astype(jnp.float32) + rms_norm(mlp_proj, post_gain[1])).astype(jnp.bfloat16)
+    return mlp(mid_state, w_gate_up, w_down, post_gain[1:2], lax.axis_size("blk"))
 
 
 def solution(mesh):

time: 316 us -> 255 us (0.81)
  waiting for transfers between devices: 234 us -> 116 us
  Pallas kernels: 0 us -> 65.7 us
  matrix products: 29.9 us -> 19.5 us
  local copies, waits for them, and re-layouts: 13.4 us -> 17.8 us
    reduce_scatter x1 -> x0, waiting for transfers between devices: 66.7 us -> none  [on_device(): lax.psum_scatter(jnp.dot(hidden, w_down, preferred_element_type=jnp.float...]
    pallas_call x0 -> x1, Pallas kernels: none -> 65.7 us  [mlp(): pl.pallas_call(functools.partial(mlp_kernel, lines), out_shape=jax.ShapeD...]
    all_gather x1 -> x0, waiting for transfers between devices: 49.8 us -> none  [on_device(): lax.all_gather(mid_state, 'blk', axis=0, tiled=True)]
    dot_general x2 -> x0, matrix products: 11.4 us -> none  [the longest x1 7.69 us: on_device(): jnp.einsum('rd,cdf->crf', lax.all_gather(mid_state, 'blk', axis=0, tiled=...]
  transfers between devices with their start and end apart: 5 -> 3, of which waited for: 5 -> 3; matrix products, arithmetic and copies ran while one was open for 4% -> 6% of each run, Pallas kernels for 0% -> 0%
where the time goes in v1:
time: 255 us; the launch traced here: 253 us
  waiting for transfers between devices  116 us (45%)
  Pallas kernels  65.7 us (26%)
  matrix products  19.5 us (8%)
  local copies, waits for them, and re-layouts  17.8 us (7%)
  between operations  14 us (5%)
  other arithmetic  11.9 us (5%)
  blocking collectives  8.49 us (3%)
    pallas_call x1, Pallas kernels, mlp(): pl.pallas_call(functools.partial(mlp_kernel, lines), out_shape=jax.ShapeD...  65.7 us
    all_gather x1, waiting for transfers between devices, on_device(): values_piece = lax.all_gather(cache_values, 'blk', axis=0, tiled=True)  49.9 us
    psum x1, waiting for transfers between devices, on_device(): lax.psum(attn_part.astype(jnp.bfloat16), 'head').astype(jnp.float32)  34.1 us
    all_gather x1, waiting for transfers between devices, on_device(): keys_piece = lax.all_gather(cache_keys, 'blk', axis=0, tiled=True)  30.6 us
    dot_general x2, matrix products, masked_partial(): jnp.einsum('rhk,khe->rhe', weights.astype(jnp.bfloat16), values_in, prefe...  9.26 us
    psum x1, blocking collectives, on_device(): lax.psum((jnp.sum(qkv_raw[0] * qkv_raw[0], axis=1), jnp.sum(qkv_raw[1] *...  8.49 us
  transfers between devices with their start and end apart: 3, of which 3 were waited for; matrix products, arithmetic and copies ran while one was open for 6% of the time, Pallas kernels for 0%

profile of v1, /device:TPU:0, one launch (start us, length us, event | category | flops | bytes accessed | tf_op | source)
XLA Modules:
  0.0 253.5 jit_solution(6987101653490908430)
XLA Ops:
  6.5 0.7 all-gather.3.cloned.1.call-update
  7.3 0.0 all-gather.5.cloned.1.call-start
  7.3 0.7 all-gather.5.cloned.1.call-update
  8.0 0.0 all-reduce.3.cloned.1.call-start
  8.1 0.9 convert_reduce_fusion
  9.0 0.2 reduce_window_sum.11
  9.2 5.0 %convolution_bitcast_fusion = f32[3,256,512]{1,2,0:T(8,128)S(1)} fusion(bf16[3,2048,512]{2,1,0:T(8,128)(2,1)} %param.17, bf16[256,2048]{1,0:T(8,128)(2,1)} %param.16), kind=kOutput, calls=%fused_computation.26 | convolution fusion | flops 1610612736 | bytes 8912896 | tf_op jit(solution)/shard_map/td,cdw->ctw/dot_general | solution.py:307
  14.2 0.7 slice.67
  14.9 0.1 multiply_reduce_fusion.1
  15.0 1.0 copy.49
  16.0 0.2 copy.48
  16.3 0.1 select_reduce_fusion.1
  16.4 0.1 select_reduce_fusion.5
  16.5 0.7 or_reduce_fusion
  17.8 8.5 %all-reduce = (f32[256]{0:T(256)S(1)}, f32[256]{0:T(256)S(1)}) all-reduce(f32[256]{0:T(256)S(1)} %get-tuple-element.109, f32[256]{0:T(256)S(1)} %get-tuple-element.108), channel_id=1, replica_groups=mesh['blk'=8,'head'=4] {'head'}, use_global_device_ids=true, to_apply=%region_11.12 | all-reduce | flops 512 | bytes 4096 | tf_op jit(solution)/shard_map/psum | solution.py:308
  26.3 0.1 select_reduce_fusion.3
  26.5 0.5 multiply_cosine_fusion
  27.0 1.2 multiply_multiply_fusion
  28.2 0.1 multiply_multiply_fusion.1
  28.3 0.4 subtract_convert_fusion.1
  28.8 0.1 pad_maximum_fusion
  28.9 0.1 fusion.45
  29.0 0.4 fusion.56
  29.4 0.2 fusion.33
  29.6 1.3 convolution_bitcast_fusion.1
  30.9 30.6 %all-gather.3.cloned.1.call-done = bf16[8,256,512]{2,1,0:T(8,128)(2,1)} async-done(((bf16[1,256,512]{2,1,0:T(8,128)(2,1)}), bf16[8,256,512]{2,1,0:T(8,128)(2,1)}) %all-gather.3.cloned.1.call-update) | async-done | bytes 2097168 | tf_op jit(solution)/shard_map/all_gather | solution.py:332
  61.5 49.9 %all-gather.5.cloned.1.call-done = bf16[8,256,512]{2,1,0:T(8,128)(2,1)} async-done(((bf16[1,256,512]{2,1,0:T(8,128)(2,1)}), bf16[8,256,512]{2,1,0:T(8,128)(2,1)}) %all-gather.5.cloned.1.call-update) | async-done | bytes 2097168 | tf_op jit(solution)/shard_map/all_gather | solution.py:333
  111.5 28.5 %conditional.1 = ((f32[256,4]{0,1:T(4,128)S(1)}, f32[256,4,128]{0,2,1:T(8,128)S(1)})) conditional(s32[]{:T(128)} %convert_element_type.46, (f32[256,4]{0,1:T(4,128)S(1)}, f32[256,4,128]{0,2,1:T(8,128)S(1)}) %tuple.12, (s32[8]{0:T(128)S(1)}, s32[256]{0:T(256)S(1)}, s32[256]{0:T(256)S(1)}, s32[8,8]{1,0:T(8,128)S(1)}, s32[8]{0:T(128)S(1)}, ...), branch_computations={%region_14.15_spmd, %region_15.19_spmd} | conditional | flops 1103501568 | bytes 76904920 | solution.py:350
  111.5 0.1 broadcast_bitcast_fusion
  111.5 0.2 select_reduce_fusion
  111.7 0.1 iota_compare_fusion
  111.8 1.5 or_and_fusion
  113.3 4.0 %reshape.247 = bf16[2048,4,128]{2,1,0:T(4,128)(2,1)} reshape(bf16[8,256,512]{2,1,0:T(8,128)(2,1)} %get-tuple-element.47) | data formatting | bytes 4194304 | tf_op jit(solution)/shard_map/cond/branch_1_fun/reshape | solution.py:269
  117.3 3.1 %fusion = (f32[256,4]{0,1:T(4,128)S(1)}, f32[4,2048,256]{2,1,0:T(8,128)S(1)}) fusion(pred[256,2048]{0,1:T(8,128)(4,1)S(1)} %or_and_fusion, bf16[256,4,128]{2,0,1:T(8,128)(2,1)S(1)} %get-tuple-element.48, bf16[2048,4,128]{2,1,0:T(4,128)(2,1)} %reshape.247), kind=kOutput, calls=%fused_computation.2 | convolution fusion | flops 543161344 | bytes 11276288 | tf_op jit(solution)/shard_map/cond/branch_1_fun/rhe,khe->rhk/dot_general | solution.py:279
  120.4 3.2 %copy-done.1 = f32[4,2048,256]{2,1,0:T(8,128)} copy-done((f32[4,2048,256]{2,1,0:T(8,128)}, f32[4,2048,256]{2,1,0:T(8,128)S(1)}, u32[]{:S(2)}) %copy-start.1) | copy-done | bytes 8388632 | tf_op jit(solution)/shard_map/cond
  123.6 2.1 fusion.2
  125.7 4.0 %reshape.248 = bf16[2048,4,128]{2,1,0:T(4,128)(2,1)} reshape(bf16[8,256,512]{2,1,0:T(8,128)(2,1)} %get-tuple-element.50) | data formatting | bytes 4194304 | tf_op jit(solution)/shard_map/cond/branch_1_fun/reshape | solution.py:270
  129.7 1.0 copy.52
  130.7 8.0 %fusion.19 = f32[256,4,128]{2,0,1:T(8,128)} fusion(bf16[2048,4,128]{2,1,0:T(4,128)(2,1)} %reshape.248, f32[4,2048,256]{2,1,0:T(8,128)} %copy-done.1, f32[256,4]{0,1:T(4,128)S(1)} %get-tuple-element.119, pred[256,2048]{0,1:T(8,128)(4,1)S(1)} %or_and_fusion, f32[256,4,128]{2,0,1:T(8,128)} %copy.52, f32[256,4]{0,1:T(4,128)S(1)} %get-tuple-element.118, ...), kind=kOutput, calls=%fused_computation.13 | convolution fusion | flops 547749888 | bytes 12070912 | tf_op jit(solution)/shard_map/cond/branch_1_fun/rhk,khe->rhe/dot_general | solution.py:251
  138.7 1.2 copy.58
  140.0 1.8 convolution_convert_fusion
  141.8 0.0 all-reduce.3.cloned.1.call-update
  141.8 0.6 fusion.54
  142.4 34.1 %all-reduce.3.cloned.1.call-done = bf16[256,2048]{1,0:T(8,128)(2,1)} async-done(((bf16[256,2048]{1,0:T(8,128)(2,1)}), bf16[256,2048]{1,0:T(8,128)(2,1)}) %all-reduce.3.cloned.1.call-update) | async-done | bytes 1048592 | tf_op jit(solution)/shard_map/psum | solution.py:356
  176.5 1.1 fusion.37
  177.6 1.9 fusion.36.mid_ref
  179.5 65.7 %shard_map.136 = bf16[64,2048]{1,0:T(8,128)(2,1)} custom-call(bf16[64,2048]{1,0:T(8,128)(2,1)} %fusion.36.mid_ref, bf16[2,2048,1024]{2,1,0:T(8,128)(2,1)} %wgu_hbm.1, bf16[1024,2048]{1,0:T(8,128)(2,1)} %wd_hbm.1, f32[1,2048]{1,0:T(1,128)} %get-tuple-element.129.gain_ref), custom_call_target="tpu_custom_call" | custom-call | tf_op jit(solution)/shard_map/pallas_call | solution.py:173
  245.3 1.7 copy.78
  (31 shorter events, 0.2 us)
Async XLA Ops:
  6.5 133.5 %copy-start = (bf16[512,2048]{1,0:T(8,128)(2,1)S(1)}, bf16[512,2048]{1,0:T(8,128)(2,1)}, u32[]{:S(2)}) copy-start(bf16[512,2048]{1,0:T(8,128)(2,1)} %param.19) | copy-start | bytes 6291460
  6.5 55.0 %all-gather.3.cloned.1.call-start = ((), (), s32[]{:S(2)}) async-start(), calls=%async_computation | async-start | bytes 2359296 | tf_op jit(solution)/shard_map/all_gather | solution.py:332
  7.3 104.2 %all-gather.5.cloned.1.call-start = ((), (), s32[]{:S(2)}) async-start(), calls=%async_computation.1 | async-start | bytes 2359296 | tf_op jit(solution)/shard_map/all_gather | solution.py:333
  8.0 168.5 %all-reduce.3.cloned.1.call-start = ((), (), s32[]{:S(2)}) async-start(), calls=%async_computation.2 | async-start | bytes 2097152 | tf_op jit(solution)/shard_map/psum | solution.py:356
  9.1 7.1 %copy-start.2 = (s32[8,256]{1,0:T(8,128)S(1)}, s32[8,256]{1,0:T(8,128)}, u32[]{:S(2)}) copy-start(s32[8,256]{1,0:T(8,128)} %param.28) | copy-start | bytes 24580
  9.1 7.1 %copy-start.6 = (s32[8,8]{1,0:T(8,128)S(1)}, s32[8,8]{1,0:T(8,128)}, u32[]{:S(2)}) copy-start(s32[8,8]{1,0:T(8,128)} %param.29) | copy-start | bytes 772
  9.1 7.2 %copy-start.8 = (s32[4]{0:T(128)S(1)}, s32[4]{0:T(128)}, u32[]{:S(2)}) copy-start(s32[4]{0:T(128)} %param.27) | copy-start | bytes 52
  9.1 7.3 %copy-start.4 = (s32[8]{0:T(128)S(1)}, s32[8]{0:T(128)}, u32[]{:S(2)}) copy-start(s32[8]{0:T(128)} %param.25) | copy-start | bytes 100
  9.2 17.2 %copy-start.7 = (s32[8]{0:T(128)S(1)}, s32[8]{0:T(128)}, u32[]{:S(2)}) copy-start(s32[8]{0:T(128)} %param.26) | copy-start | bytes 100
  9.2 17.3 %copy-start.5 = (f32[2,512]{1,0:T(2,128)S(1)}, f32[2,512]{1,0:T(2,128)}, u32[]{:S(2)}) copy-start(f32[2,512]{1,0:T(2,128)} %param.18) | copy-start | bytes 12292
  111.5 30.4 %copy-start.3 = (f32[2,2048]{1,0:T(2,128)S(1)}, f32[2,2048]{1,0:T(2,128)}, u32[]{:S(2)}) copy-start(f32[2,2048]{1,0:T(2,128)} %param.20) | copy-start | bytes 49156
  120.4 3.2 %copy-start.1 = (f32[4,2048,256]{2,1,0:T(8,128)}, f32[4,2048,256]{2,1,0:T(8,128)S(1)}, u32[]{:S(2)}) copy-start(f32[4,2048,256]{2,1,0:T(8,128)S(1)} %get-tuple-element.120) | copy-start | bytes 25165828 | tf_op jit(solution)/shard_map/cond
Sparse Core Ops, SparseCore 0:
  9.5 51.9 all-gather.2
  63.6 47.7 all-gather.4
  141.9 34.5 all-reduce.2

commit v2 on v1

v2 whole, which is shorter than its diff:
```python
import functools

import jax
import jax.numpy as jnp
from jax import lax
from jax.experimental import pallas as pl
from jax.experimental.pallas import tpu as pltpu
from jax.sharding import PartitionSpec as P

HD = 128
EPS = 1e-06
THETA = 500000.0
NEG = -1e30
MESH = pl.DeviceIdType.MESH
BF16 = jnp.bfloat16
F32 = jnp.float32


def by_distance(at, count, step):
    back = count - 1 - at
    near = jnp.minimum(at, back)
    both = jnp.where(step % 2 == 1, at - (step + 1) // 2, at + step // 2)
    return jnp.where(step <= 2 * near, both, jnp.where(at < back, step, count - 1 - step))


def remote(src, dst, send_sem, recv_sem, **where):
    return pltpu.make_async_remote_copy(
        src_ref=src,
        dst_ref=dst,
        send_sem=send_sem,
        recv_sem=recv_sem,
        device_id=where,
        device_id_type=MESH,
    )


def meet(peers):
    barrier = pltpu.get_barrier_semaphore()
    for peer in peers:
        pl.semaphore_signal(barrier, inc=1, device_id=peer, device_id_type=MESH)
    pl.semaphore_wait(barrier, len(peers))


def mlp_kernel(
    lines,
    mid_ref, wgu_hbm, wd_hbm, gain_ref, out_ref,
    gathered, wgu, wd, hidden, whole, own_part, send_x, recv_x, send_z, recv_z,
    w_sem, g_send, g_recv, x_send, x_recv, z_send, z_recv,
):
    rows, width = mid_ref.shape
    units = wd.shape[0]
    me = lax.axis_index("blk")
    z, x = me // 2, me % 2
    other = z * 2 + 1 - x

    loads = [
        pltpu.make_async_copy(wgu_hbm.at[0], wgu.at[0], w_sem.at[0]),
        pltpu.make_async_copy(wgu_hbm.at[1], wgu.at[1], w_sem.at[1]),
        pltpu.make_async_copy(wd_hbm, wd, w_sem.at[2]),
    ]
    for load in loads:
        load.start()
    meet([{"blk": other}] + [{"blk": (z + j) % lines * 2 + x} for j in range(1, lines)])

    def block(index):
        return gathered.at[pl.ds(pl.multiple_of(index * rows, rows), rows)]

    def pass_on(index, way, target):
        return remote(block(index), block(index), g_send.at[way, index], g_recv.at[index], blk=target)

    def spread(origin, wait):
        index = origin * 2 + x
        if wait:
            pass_on(index, 0, other).wait_recv()
        pass_on(index, 0, other).start()

        @pl.when((origin <= z) & (z < lines - 1))
        def _():
            pass_on(index, 1, me + 2).start()

        @pl.when((origin >= z) & (z > 0))
        def _():
            pass_on(index, 2, me - 2).start()

    gathered[pl.ds(pl.multiple_of(me * rows, rows), rows), :] = mid_ref[...]
    spread(z, False)

    def to_x(origin):
        return remote(send_x.at[origin], recv_x.at[origin], x_send.at[origin], x_recv.at[origin], blk=other)

    def to_z(origin):
        return remote(send_z.at[origin], recv_z.at[z], z_send.at[origin], z_recv.at[z], blk=origin * 2 + x)

    def reduce_x(origin):
        to_x(origin).wait_recv()
        summed = own_part[origin] + recv_x[origin].astype(F32)
        own_part[origin] = summed
        send_z[origin] = summed.astype(BF16)

        @pl.when(origin != z)
        def _():
            to_z(origin).start()

    tile = min(256, units)
    wide = min(512, width)
    for step in range(lines):
        origin = by_distance(z, lines, step)
        if step + 1 < lines:
            spread(by_distance(z, lines, step + 1), True)
        pass_on(origin * 2 + 1 - x, 0, other).wait_recv()
        if step == 0:
            loads[0].wait()
            loads[1].wait()
        chunk = pl.ds(pl.multiple_of(origin * 2 * rows, 2 * rows), 2 * rows)

        @pl.loop(0, units // tile)
        def _(t):
            at = pl.ds(pl.multiple_of(t * tile, tile), tile)
            state = gathered[chunk, :]
            gate = jnp.dot(state, wgu[0, :, at], preferred_element_type=F32)
            up = jnp.dot(state, wgu[1, :, at], preferred_element_type=F32)
            hidden[:, at] = (gate / (1.0 + jnp.exp(-gate)) * up).astype(BF16)

        if step == 0:
            loads[2].wait()

        @pl.loop(0, width // wide)
        def _(t):
            at = pl.ds(pl.multiple_of(t * wide, wide), wide)
            whole[:, at] = jnp.dot(hidden[...], wd[:, at], preferred_element_type=F32)

        own_part[origin] = whole[pl.ds(pl.multiple_of(x * rows, rows), rows), :]
        send_x[origin] = whole[pl.ds(pl.multiple_of((1 - x) * rows, rows), rows), :].astype(BF16)
        to_x(origin).start()
        if step > 0:
            reduce_x(by_distance(z, lines, step - 1))
    reduce_x(by_distance(z, lines, lines - 1))

    total = own_part[z]
    for j in range(1, lines):
        source = (z + j) % lines
        remote(send_z.at[0], recv_z.at[source], z_send.at[0], z_recv.at[source], blk=other).wait_recv()
        total = total + recv_z[source].astype(F32)
    scale = lax.rsqrt(jnp.mean(total * total, axis=-1, keepdims=True) + EPS)
    out_ref[...] = (mid_ref[...].astype(F32) + total * scale * gain_ref[...]).astype(BF16)

    for origin in range(lines):
        index = origin * 2 + x
        to_x(origin).wait_send()
        pass_on(index, 0, other).wait_send()

        @pl.when((origin <= z) & (z < lines - 1))
        def _():
            pass_on(index, 1, me + 2).wait_send()

        @pl.when((origin >= z) & (z > 0))
        def _():
            pass_on(index, 2, me - 2).wait_send()

        @pl.when(origin != z)
        def _():
            to_z(origin).wait_send()


def mlp(mid_state, w_gate_up, w_down, gain, devices):
    rows, width = mid_state.shape
    units = w_down.shape[0]
    lines = devices // 2
    vmem = pl.BlockSpec(memory_space=pltpu.VMEM)
    hbm = pl.BlockSpec(memory_space=pl.ANY)
    dma = pltpu.SemaphoreType.DMA
    part = pltpu.VMEM((lines, rows, width), BF16)
    return pl.pallas_call(
        functools.partial(mlp_kernel, lines),
        out_shape=jax.ShapeDtypeStruct((rows, width), BF16),
        in_specs=[vmem, hbm, hbm, vmem],
        out_specs=vmem,
        scratch_shapes=[
            pltpu.VMEM((devices * rows, width), BF16),
            pltpu.VMEM(w_gate_up.shape, BF16),
            pltpu.VMEM(w_down.shape, BF16),
            pltpu.VMEM((2 * rows, units), BF16),
            pltpu.VMEM((2 * rows, width), F32),
            pltpu.VMEM((lines, rows, width), F32),
            part, part, part, part,
            dma((3,)),
            dma((3, devices)),
            dma((devices,)),
            dma((lines,)),
            dma((lines,)),
            dma((lines,)),
            dma((lines,)),
        ],
        compiler_params=pltpu.CompilerParams(
            collective_id=1, has_side_effects=True, vmem_limit_bytes=60 * 2**20
        ),
    )(mid_state, w_gate_up, w_down, gain)


def attention_kernel(
    spread_count,
    states_ref, wqkv_hbm, gain_ref, cos_ref, sin_ref, first_ref, limit_ref, keys_hbm, values_hbm,
    wout_hbm, post_ref, out_ref,
    wqkv, wout, raw, query, key, value, squares, query_in, keys_in, values_in,
    peak, norm, acc, leaf_peak, leaf_norm, leaf_acc, part_out, part_in, stat_out, stat_in,
    attended, proj, proj_low, pair_in, pair_out, line_in,
    w_sem, s_send, s_recv, q_send, q_recv, own_sem, k_send, k_recv, v_send, v_recv,
    p_send, p_recv, t_send, t_recv, c_send, c_recv, y_send, y_recv,
):
    rows, width = states_ref.shape
    heads = query.shape[0]
    node_rows = keys_hbm.shape[1]
    slots = keys_in.shape[0]
    me = lax.axis_index("blk")
    head = lax.axis_index("head")
    mine, rest = me // spread_count, me % spread_count
    scale = HD ** (-0.5)

    loads = [pltpu.make_async_copy(wqkv_hbm.at[c], wqkv.at[c], w_sem.at[c]) for c in range(3)]
    loads.append(pltpu.make_async_copy(wout_hbm, wout, w_sem.at[3]))
    for load in loads:
        load.start()

    def holder(index):
        return index * spread_count + rest

    peers = [{"head": (head + j) % 4} for j in range(1, 4)]
    peers += [{"blk": holder((mine + j) % heads)} for j in range(1, heads)]
    peers += [{"blk": mine * spread_count + (rest + j) % spread_count} for j in range(1, spread_count)]
    meet(peers)

    def column(index):
        return pl.ds(pl.multiple_of(index * HD, HD), HD)

    def cache_out(target):
        return (
            remote(keys_hbm.at[0, :, column(target)], keys_in.at[me], k_send.at[0, target], k_recv.at[me], blk=holder(target)),
            remote(values_hbm.at[0, :, column(target)], values_in.at[me], v_send.at[0, target], v_recv.at[me], blk=holder(target)),
        )

    def cache_wait(slot):
        far = holder((mine + 1) % heads)
        remote(keys_in.at[slot], keys_in.at[slot], k_send.at[0, 0], k_recv.at[slot], blk=far).wait_recv()
        remote(values_in.at[slot], values_in.at[slot], v_send.at[0, 0], v_recv.at[slot], blk=far).wait_recv()

    def cache_on(source, j):
        slot = holder(source)
        target = mine * spread_count + (rest + j) % spread_count
        return (
            remote(keys_in.at[slot], keys_in.at[slot], k_send.at[j, source], k_recv.at[slot], blk=target),
            remote(values_in.at[slot], values_in.at[slot], v_send.at[j, source], v_recv.at[slot], blk=target),
        )

    for j in range(1, heads):
        for copy in cache_out((mine + j) % heads):
            copy.start()
    own_copies = [
        pltpu.make_async_copy(keys_hbm.at[0, :, column(mine)], keys_in.at[me], own_sem.at[0]),
        pltpu.make_async_copy(values_hbm.at[0, :, column(mine)], values_in.at[me], own_sem.at[1]),
    ]
    for copy in own_copies:
        copy.start()

    def pass_on(step):
        source = by_distance(mine, heads, step)
        if step == 0:
            for copy in own_copies:
                copy.wait()
        else:
            cache_wait(holder(source))
        for j in range(1, spread_count):
            for copy in cache_on(source, j):
                copy.start()

    tile = 2 * HD
    here = heads * HD

    def product(c):
        loads[c].wait()

        @pl.loop(0, here // tile)
        def _(t):
            at = pl.ds(pl.multiple_of(t * tile, tile), tile)
            raw[c, :, at] = jnp.dot(states_ref[...], wqkv[c, :, at], preferred_element_type=F32)

    lane = lax.broadcasted_iota(jnp.int32, (rows, HD), 1)
    product(0)
    pass_on(0)
    product(1)
    query_sum = jnp.sum(raw[0] * raw[0], axis=-1, keepdims=True)
    key_sum = jnp.sum(raw[1] * raw[1], axis=-1, keepdims=True)
    packed = jnp.where(lane == 0, query_sum, jnp.where(lane == 1, key_sum, 0.0))
    squares[head] = jnp.transpose(packed)[0:8]

    def squares_to(target):
        return remote(squares.at[head], squares.at[head], s_send.at[target], s_recv.at[head], head=target)

    for j in range(1, 4):
        squares_to((head + j) % 4).start()
    product(2)
    value[...] = raw[2].astype(BF16)
    pass_on(1)
    total = squares[head]
    for j in range(1, 4):
        source = (head + j) % 4
        remote(squares.at[source], squares.at[source], s_send.at[source], s_recv.at[source], head=source).wait_recv()
        total = total + squares[source]
    spread = jnp.transpose(jnp.concatenate([total] * (HD // 8), axis=0))
    scales = lax.rsqrt(spread / width + EPS)
    query_scale, key_scale = scales[:, 0:1], scales[:, 1:2]

    def turned(c, h, by):
        at = slice(h * HD, (h + 1) * HD)
        normed = raw[c, :, at] * by * gain_ref[c : c + 1, at]
        swapped = pltpu.roll(normed, HD // 2, 1)
        return (normed * cos_ref[...] + swapped * sin_ref[...]).astype(BF16)

    for h in range(heads):
        query[h] = turned(0, h, query_scale)

    def query_to(target):
        return remote(query.at[target], query_in.at[mine], q_send.at[target], q_recv.at[mine], blk=holder(target))

    for j in range(1, heads):
        query_to((mine + j) % heads).start()
    query_in[mine] = query[mine]
    for h in range(heads):
        key[h] = turned(1, h, key_scale)
    pass_on(2)

    row_at = lax.broadcasted_iota(jnp.int32, (rows, rows), 0)
    key_at = lax.broadcasted_iota(jnp.int32, (rows, rows), 1)
    see_leaf = (key_at >= first_ref[...]) & (key_at <= row_at)
    over = (((1,), (1,)), ((), ()))
    for h in range(heads):
        scores = lax.dot_general(query[h], key[h], over, preferred_element_type=F32) * scale
        scores = jnp.where(see_leaf, scores, NEG)
        top = jnp.max(scores, axis=-1, keepdims=True)
        weights = jnp.exp(scores - top)
        leaf_peak[h] = jnp.broadcast_to(top, (rows, HD))
        leaf_norm[h] = jnp.broadcast_to(jnp.sum(weights, axis=-1, keepdims=True), (rows, HD))
        leaf_acc[h] = jnp.dot(weights.astype(BF16), value[:, h * HD : (h + 1) * HD], preferred_element_type=F32)
        if h == 1:
            for step in range(3, heads):
                pass_on(step)

    for j in range(1, heads):
        source = (mine + j) % heads
        remote(query.at[0], query_in.at[source], q_send.at[0], q_recv.at[source], blk=holder(source)).wait_recv()
    peak[...] = jnp.full(peak.shape, NEG, F32)
    norm[...] = jnp.zeros(norm.shape, F32)
    acc[...] = jnp.zeros(acc.shape, F32)
    key_row = lax.broadcasted_iota(jnp.int32, (rows, node_rows), 1)
    slot_lane = lax.broadcasted_iota(jnp.int32, (rows, slots), 1)

    def look_at(slot):
        @pl.loop(0, heads)
        def _(g):
            limit = jnp.max(jnp.where(slot_lane == slot, limit_ref[g], 0), axis=-1, keepdims=True)
            scores = lax.dot_general(query_in[g], keys_in[slot], over, preferred_element_type=F32) * scale
            scores = jnp.where(key_row < limit, scores, NEG)
            before = peak[g]
            top = jnp.maximum(before, jnp.max(scores, axis=-1, keepdims=True))
            weights = jnp.exp(scores - top[:, 0:1])
            shrink = jnp.exp(before - top)
            peak[g] = top
            norm[g] = norm[g] * shrink + jnp.sum(weights, axis=-1, keepdims=True)
            acc[g] = acc[g] * shrink + jnp.dot(
                weights.astype(BF16), values_in[slot], preferred_element_type=F32
            )

    for step in range(heads):
        look_at(holder(by_distance(mine, heads, step)))
    for step in range(heads):
        for j in range(1, spread_count):
            slot = by_distance(mine, heads, step) * spread_count + (rest + j) % spread_count
            cache_wait(slot)
            look_at(slot)

    def part_to(target):
        return (
            remote(part_out.at[target], part_in.at[mine], p_send.at[target], p_recv.at[mine], blk=holder(target)),
            remote(stat_out.at[target], stat_in.at[mine], t_send.at[target], t_recv.at[mine], blk=holder(target)),
        )

    for j in list(range(1, heads)) + [0]:
        g = (mine + j) % heads
        part_out[g] = (acc[g] / norm[g]).astype(BF16)
        stats = jnp.where(lane == 0, peak[g], jnp.where(lane == 1, norm[g], 0.0))
        stat_out[g] = jnp.transpose(stats)[0:8]
        if j > 0:
            for copy in part_to(g):
                copy.start()
        else:
            part_in[g] = part_out[g]
            stat_in[g] = stat_out[g]
    for j in range(1, heads):
        source = (mine + j) % heads
        remote(part_out.at[0], part_in.at[source], p_send.at[0], p_recv.at[source], blk=holder(source)).wait_recv()
        remote(stat_out.at[0], stat_in.at[source], t_send.at[0], t_recv.at[source], blk=holder(source)).wait_recv()
    for h in range(heads):
        stats = jnp.transpose(jnp.concatenate([stat_in[h]] * (HD // 8), axis=0))
        other_peak, other_norm = stats[:, 0:1], stats[:, 1:2]
        top = jnp.maximum(leaf_peak[h], other_peak)
        own_scale = jnp.exp(leaf_peak[h] - top)
        other_scale = jnp.exp(other_peak - top) * other_norm
        summed = leaf_acc[h] * own_scale + part_in[h].astype(F32) * other_scale
        attended[:, h * HD : (h + 1) * HD] = (
            summed / (leaf_norm[h] * own_scale + other_scale)
        ).astype(BF16)

    loads[3].wait()
    wide = min(512, width)

    @pl.loop(0, width // wide)
    def _(t):
        at = pl.ds(pl.multiple_of(t * wide, wide), wide)
        tiled = jnp.dot(attended[...], wout[:, at], preferred_element_type=F32)
        proj[:, at] = tiled
        proj_low[:, at] = tiled.astype(BF16)

    y, core = head // 2, head % 2
    own_rows = out_ref.shape[0]
    sibling, across = y * 2 + 1 - core, (1 - y) * 2 + core

    def rows_of(index):
        return pl.ds(pl.multiple_of(index * own_rows, own_rows), own_rows)

    def to_pair(half):
        return remote(proj_low.at[rows_of(half * 2 + 1 - core)], pair_in.at[half], c_send.at[half], c_recv.at[half], head=sibling)

    to_pair(1 - y).start()
    to_pair(y).start()
    to_pair(1 - y).wait_recv()
    pair_out[...] = (proj[rows_of(across), :] + pair_in[1 - y].astype(F32)).astype(BF16)
    over_y = remote(pair_out, line_in, y_send.at[0], y_recv.at[0], head=across)
    over_y.start()
    to_pair(y).wait_recv()
    total = proj[rows_of(head), :] + pair_in[y].astype(F32)
    over_y.wait_recv()
    total = total + line_in[...].astype(F32)
    shrink = lax.rsqrt(jnp.mean(total * total, axis=-1, keepdims=True) + EPS)
    own = states_ref[rows_of(head), :].astype(F32)
    out_ref[...] = (own + total * shrink * post_ref[...]).astype(BF16)

    over_y.wait_send()
    for half in range(2):
        to_pair(half).wait_send()
    for j in range(1, 4):
        squares_to((head + j) % 4).wait_send()
    for j in range(1, heads):
        target = (mine + j) % heads
        query_to(target).wait_send()
        for copy in cache_out(target) + part_to(target):
            copy.wait_send()
    for source in range(heads):
        for j in range(1, spread_count):
            for copy in cache_on(source, j):
                copy.wait_send()


def attention(states_in, w_qkv, qk_gain, cosine, sine, first, limits, cache_keys, cache_values, w_out, gain, slots):
    rows, width = states_in.shape
    here = w_qkv.shape[2]
    heads = here // HD
    node_rows = cache_keys.shape[1]
    own_rows = rows // 4
    vmem = pl.BlockSpec(memory_space=pltpu.VMEM)
    hbm = pl.BlockSpec(memory_space=pl.ANY)
    dma = pltpu.SemaphoreType.DMA
    spread_count = slots // heads

    def per_head(kind):
        return pltpu.VMEM((heads, rows, HD), kind)

    return pl.pallas_call(
        functools.partial(attention_kernel, spread_count),
        out_shape=jax.ShapeDtypeStruct((own_rows, width), BF16),
        in_specs=[vmem, hbm, vmem, vmem, vmem, vmem, vmem, hbm, hbm, hbm, vmem],
        out_specs=vmem,
        scratch_shapes=[
            pltpu.VMEM(w_qkv.shape, BF16),
            pltpu.VMEM(w_out.shape, BF16),
            pltpu.VMEM((3, rows, here), F32),
            per_head(BF16),
            per_head(BF16),
            pltpu.VMEM((rows, here), BF16),
            pltpu.VMEM((4, 8, rows), F32),
            per_head(BF16),
            pltpu.VMEM((slots, node_rows, HD), BF16),
            pltpu.VMEM((slots, node_rows, HD), BF16),
            per_head(F32), per_head(F32), per_head(F32),
            per_head(F32), per_head(F32), per_head(F32),
            per_head(BF16), per_head(BF16),
            pltpu.VMEM((heads, 8, rows), F32),
            pltpu.VMEM((heads, 8, rows), F32),
            pltpu.VMEM((rows, here), BF16),
            pltpu.VMEM((rows, width), F32),
            pltpu.VMEM((rows, width), BF16),
            pltpu.VMEM((2, own_rows, width), BF16),
            pltpu.VMEM((own_rows, width), BF16),
            pltpu.VMEM((own_rows, width), BF16),
            dma((4,)),
            dma((4,)), dma((4,)),
            dma((heads,)), dma((heads,)),
            dma((2,)),
            dma((spread_count, heads)), dma((slots,)),
            dma((spread_count, heads)), dma((slots,)),
            dma((heads,)), dma((heads,)),
            dma((heads,)), dma((heads,)),
            dma((2,)), dma((2,)),
            dma((1,)), dma((1,)),
        ],
        compiler_params=pltpu.CompilerParams(
            collective_id=2, has_side_effects=True, vmem_limit_bytes=60 * 2**20
        ),
    )(states_in, w_qkv, qk_gain, cosine, sine, first, limits, cache_keys, cache_values, w_out, gain)


def on_device(
    states_in,
    w_qkv,
    qk_gain,
    w_out,
    post_gain,
    w_gate_up,
    w_down,
    cache_keys,
    cache_values,
    slot_node,
    node_length,
    node_parent,
    leaf_segment,
    leaf_node,
):
    blk_index = lax.axis_index("blk")
    devices = lax.axis_size("blk")
    heads = w_qkv.shape[2] // HD
    spread_count = devices // heads
    mine, rest = blk_index // spread_count, blk_index % spread_count
    tok_rows = leaf_segment.shape[1]
    leaves = leaf_node.shape[1]
    middles = node_parent.shape[0]
    nodes = node_length.shape[0]
    segments = lax.dynamic_index_in_dim(leaf_segment.reshape(heads, spread_count, tok_rows), rest, 1, keepdims=False)
    hangs = lax.dynamic_index_in_dim(leaf_node.reshape(heads, spread_count, leaves), rest, 1, keepdims=False)
    node_ids = jnp.arange(nodes, dtype=jnp.int32)
    middle_ids = jnp.arange(middles, dtype=jnp.int32) + (nodes - middles)
    roots = jnp.sum(jnp.where(hangs[..., None] == middle_ids, node_parent, 0), axis=-1)
    lengths = jnp.sum(jnp.where(slot_node[:, None] == node_ids[None, :], node_length[None, :], 0), axis=-1)
    seen = (slot_node == hangs[..., None]) | (slot_node == roots[..., None])
    leaf_limits = jnp.where(seen, lengths, 0)
    leaf_ids = jnp.arange(leaves, dtype=jnp.int32)
    onehot = segments[:, :, None] == leaf_ids
    limits = jnp.sum(jnp.where(onehot[..., None], leaf_limits[:, None], 0), axis=2)
    segment = lax.dynamic_index_in_dim(segments, mine, 0, keepdims=False)
    first = jnp.sum((segment[None, :] < segment[:, None]).astype(jnp.int32), axis=-1)
    before = jnp.sum(lax.dynamic_index_in_dim(limits, mine, 0, keepdims=False), axis=-1)
    position = before + jnp.arange(tok_rows, dtype=jnp.int32) - first
    half = HD // 2
    frequency = THETA ** (-2.0 * jnp.arange(half, dtype=F32) / HD)
    angles = position.astype(F32)[:, None] * frequency[None, :]
    cosine, sine = jnp.cos(angles), jnp.sin(angles)
    mid_state = attention(
        states_in,
        w_qkv,
        qk_gain,
        jnp.concatenate([cosine, cosine], axis=-1),
        jnp.concatenate([-sine, sine], axis=-1),
        first[:, None],
        limits,
        cache_keys,
        cache_values,
        w_out,
        post_gain[0:1],
        devices,
    )
    return mlp(mid_state, w_gate_up, w_down, post_gain[1:2], devices)


def solution(mesh):
    placed = (
        P("blk", None),
        P(None, None, "head"),
        P(None, "head"),
        P("head", None),
        P(),
        P(None, None, "blk"),
        P("blk", None),
        P("blk", None, "head"),
        P("blk", None, "head"),
        P(),
        P(),
        P(),
        P(),
        P(),
    )
    return jax.shard_map(
        on_device, mesh=mesh, in_specs=placed, out_specs=P(("blk", "head"), None), check_vma=False
    )
```

time: 255 us -> 142 us (0.56)
  waiting for transfers between devices: 116 us -> 0 us
  Pallas kernels: 65.7 us -> 129 us
  matrix products: 19.5 us -> 0 us
  between operations: 14 us -> 0.07 us
  local copies, waits for them, and re-layouts: 17.8 us -> 6.3 us
  blocking collectives: 8.49 us -> 0 us
  other arithmetic: 11.9 us -> 4.03 us
    all_gather x2 -> x0, waiting for transfers between devices: 80.5 us -> none  [the longest x1 49.9 us: on_device(): values_piece = lax.all_gather(cache_values, 'blk', axis=0, tiled=True)]
    pallas_call x0 -> x1, Pallas kernels: none -> 59.6 us  [attention(): pl.pallas_call(functools.partial(attention_kernel, spread_count), out_sha...]
    psum x1 -> x0, waiting for transfers between devices: 34.1 us -> none  [on_device(): lax.psum(attn_part.astype(jnp.bfloat16), 'head').astype(jnp.float32)]
    dot_general x6 -> x0, matrix products: 19.5 us -> none  [the longest x2 9.26 us: masked_partial(): jnp.einsum('rhk,khe->rhe', weights.astype(jnp.bfloat16), values_in, prefe...]
    psum x1 -> x0, blocking collectives: 8.49 us -> none  [on_device(): lax.psum((jnp.sum(qkv_raw[0] * qkv_raw[0], axis=1), jnp.sum(qkv_raw[1] *...]
    reshape x2 -> x1, local copies, waits for them, and re-layouts: 7.96 us -> 0.71 us  [on_device(): leaf_segment.reshape(heads, spread_count, tok_rows)]
    cond x5 -> x0, local copies, waits for them, and re-layouts: 4.53 us -> none
    pallas_call x1, Pallas kernels: 65.7 us -> 69.1 us  [mlp(): pl.pallas_call(functools.partial(mlp_kernel, lines), out_shape=jax.ShapeD...]
  transfers between devices with their start and end apart: 3 -> 0, of which waited for: 3 -> 0; matrix products, arithmetic and copies ran while one was open for 6% -> 0% of each run, Pallas kernels for 0% -> 0%
where the time goes in v2:
time: 142 us; the launch traced here: 139 us
  Pallas kernels  129 us (91%)
  local copies, waits for them, and re-layouts  6.3 us (4%)
  other arithmetic  4.03 us (3%)
    pallas_call x1, Pallas kernels, mlp(): pl.pallas_call(functools.partial(mlp_kernel, lines), out_shape=jax.ShapeD...  69.1 us
    pallas_call x1, Pallas kernels, attention(): pl.pallas_call(functools.partial(attention_kernel, spread_count), out_sha...  59.6 us

profile of v2, /device:TPU:0, one launch (start us, length us, event | category | flops | bytes accessed | tf_op | source)
XLA Modules:
  0.0 139.1 jit_solution(3727946899187719431)
XLA Ops:
  0.0 0.0 copy-start
  0.0 0.7 copy-done
  0.7 0.9 select_reduce_fusion.2
  1.6 0.7 select_reduce_fusion.1
  2.3 0.7 reshape.45
  3.1 0.2 convert_reduce_fusion
  3.3 0.7 or_select_fusion
  4.0 0.1 select_reduce_fusion
  4.1 1.4 %fusion.1 = (f32[1,2048]{1,0:T(1,128)}, f32[1,2048]{1,0:T(1,128)}) fusion(f32[2,2048]{1,0:T(2,128)} %param.18), kind=kLoop, calls=%fused_computation.20 | loop fusion | bytes 32768 | tf_op jit(solution)/shard_map/slice | solution.py:578
  5.5 0.8 copy.16.first_ref
  6.4 0.5 fusion
  6.9 0.8 pad_maximum_fusion
  7.7 1.0 copy.17.limit_ref
  8.7 59.6 %shard_map.136.mid_ref = bf16[64,2048]{1,0:T(8,128)(2,1)} custom-call(bf16[256,2048]{1,0:T(8,128)(2,1)} %states_ref.1, bf16[3,2048,512]{2,1,0:T(8,128)(2,1)} %wqkv_hbm.1, f32[2,512]{1,0:T(2,128)} %gain_ref.1, f32[256,128]{1,0:T(8,128)} %get-tuple-element.10.cos_ref, f32[256,128]{1,0:T(8,128)} %get-tuple-element.11.sin_ref, s32[256,1]{1,0:T(8,128)} %copy.16.first_ref, ...), custom_call_target="tpu_custom_call" | custom-call | tf_op jit(solution)/shard_map/pallas_call | solution.py:476
  68.4 69.1 %shard_map.137 = bf16[64,2048]{1,0:T(8,128)(2,1)} custom-call(bf16[64,2048]{1,0:T(8,128)(2,1)} %shard_map.136.mid_ref, bf16[2,2048,1024]{2,1,0:T(8,128)(2,1)} %wgu_hbm.1, bf16[1024,2048]{1,0:T(8,128)(2,1)} %wd_hbm.1, f32[1,2048]{1,0:T(1,128)} %get-tuple-element.5.gain_ref), custom_call_target="tpu_custom_call" | custom-call | tf_op jit(solution)/shard_map/pallas_call | solution.py:173
  137.4 1.7 %copy.22 = bf16[64,2048]{1,0:T(8,128)(2,1)} copy(bf16[64,2048]{1,0:T(8,128)(2,1)} %shard_map.137) | data formatting | bytes 524288
  (9 shorter events, 0.1 us)
Async XLA Ops:
  0.0 0.7 copy-start

commit v3 on v2

v3 whole, which is shorter than its diff:
```python
import functools

import jax
import jax.numpy as jnp
from jax import lax
from jax.experimental import pallas as pl
from jax.experimental.pallas import tpu as pltpu
from jax.sharding import PartitionSpec as P

HD = 128
EPS = 1e-06
THETA = 500000.0
NEG = -1e30
MESH = pl.DeviceIdType.MESH
BF16 = jnp.bfloat16
F32 = jnp.float32


def by_distance(at, count, step):
    back = count - 1 - at
    near = jnp.minimum(at, back)
    both = jnp.where(step % 2 == 1, at - (step + 1) // 2, at + step // 2)
    return jnp.where(step <= 2 * near, both, jnp.where(at < back, step, count - 1 - step))


def remote(src, dst, send_sem, recv_sem, **where):
    return pltpu.make_async_remote_copy(
        src_ref=src,
        dst_ref=dst,
        send_sem=send_sem,
        recv_sem=recv_sem,
        device_id=where,
        device_id_type=MESH,
    )


def meet(peers):
    barrier = pltpu.get_barrier_semaphore()
    for peer in peers:
        pl.semaphore_signal(barrier, inc=1, device_id=peer, device_id_type=MESH)
    pl.semaphore_wait(barrier, len(peers))


def mlp_part(
    lines, loads,
    mid_ref, gain_ref, out_ref,
    gathered, wgu, wd, hidden, whole, own_part, own_sum, send_x, recv_x, recv_z,
    g_send, g_recv, x_send, x_recv, z_send, z_recv,
):
    rows, width = mid_ref.shape
    units = wd.shape[0]
    me = lax.axis_index("blk")
    z, x = me // 2, me % 2
    other = z * 2 + 1 - x

    def block(index):
        return gathered.at[pl.ds(pl.multiple_of(index * rows, rows), rows)]

    def pass_on(index, way, target):
        return remote(block(index), block(index), g_send.at[way, index], g_recv.at[index], blk=target)

    def spread(origin, wait):
        index = origin * 2 + x
        if wait:
            pass_on(index, 0, other).wait_recv()
        pass_on(index, 0, other).start()

        @pl.when((origin <= z) & (z < lines - 1))
        def _():
            pass_on(index, 1, me + 2).start()

        @pl.when((origin >= z) & (z > 0))
        def _():
            pass_on(index, 2, me - 2).start()

    gathered[pl.ds(pl.multiple_of(me * rows, rows), rows), :] = mid_ref[...]
    spread(z, False)

    def to_x(origin):
        return remote(send_x.at[origin], recv_x.at[origin], x_send.at[origin], x_recv.at[origin], blk=other)

    def to_z(origin):
        return remote(send_x.at[origin], recv_z.at[z], z_send.at[origin], z_recv.at[z], blk=origin * 2 + x)

    def reduce_x(step):
        origin = by_distance(z, lines, step)
        to_x(origin).wait_recv()
        summed = own_part[step % 2] + recv_x[origin].astype(F32)
        to_x(origin).wait_send()
        if step == 0:
            own_sum[...] = summed
        else:
            send_x[origin] = summed.astype(BF16)
            to_z(origin).start()

    tile = min(256, units)
    wide = min(512, width)
    for step in range(lines):
        origin = by_distance(z, lines, step)
        if step + 1 < lines:
            spread(by_distance(z, lines, step + 1), True)
        pass_on(origin * 2 + 1 - x, 0, other).wait_recv()
        if step == 0:
            loads[0].wait()
            loads[1].wait()
        chunk = pl.ds(pl.multiple_of(origin * 2 * rows, 2 * rows), 2 * rows)

        @pl.loop(0, units // tile)
        def _(t):
            at = pl.ds(pl.multiple_of(t * tile, tile), tile)
            state = gathered[chunk, :]
            gate = jnp.dot(state, wgu[0, :, at], preferred_element_type=F32)
            up = jnp.dot(state, wgu[1, :, at], preferred_element_type=F32)
            hidden[:, at] = (gate / (1.0 + jnp.exp(-gate)) * up).astype(BF16)

        if step == 0:
            loads[2].wait()

        @pl.loop(0, width // wide)
        def _(t):
            at = pl.ds(pl.multiple_of(t * wide, wide), wide)
            whole[:, at] = jnp.dot(hidden[...], wd[:, at], preferred_element_type=F32)

        own_part[step % 2] = whole[pl.ds(pl.multiple_of(x * rows, rows), rows), :]
        send_x[origin] = whole[pl.ds(pl.multiple_of((1 - x) * rows, rows), rows), :].astype(BF16)
        to_x(origin).start()
        if step > 0:
            reduce_x(step - 1)
    reduce_x(lines - 1)

    total = own_sum[...]
    for j in range(1, lines):
        source = (z + j) % lines
        remote(send_x.at[0], recv_z.at[source], z_send.at[0], z_recv.at[source], blk=other).wait_recv()
        total = total + recv_z[source].astype(F32)
    scale = lax.rsqrt(jnp.mean(total * total, axis=-1, keepdims=True) + EPS)
    out_ref[...] = (mid_ref[...].astype(F32) + total * scale * gain_ref[1:2, :]).astype(BF16)

    for origin in range(lines):
        index = origin * 2 + x
        pass_on(index, 0, other).wait_send()

        @pl.when((origin <= z) & (z < lines - 1))
        def _():
            pass_on(index, 1, me + 2).wait_send()

        @pl.when((origin >= z) & (z > 0))
        def _():
            pass_on(index, 2, me - 2).wait_send()

        @pl.when(origin != z)
        def _():
            to_z(origin).wait_send()


def layer_kernel(
    spread_count,
    states_ref, wqkv_hbm, gain_ref, wout_hbm, post_ref, wgu_hbm, wd_hbm, keys_hbm, values_hbm,
    slot_node, node_length, node_parent, segment_ref, leaf_node, frequency_ref, out_ref,
    wqkv, wout, raw, query, key, value, squares, query_in, keys_in, values_in,
    cos_ref, sin_ref, limits, own_info,
    peak, norm, acc, leaf_peak, leaf_norm, leaf_acc, part_out, part_in, stat_out, stat_in,
    attended, proj, proj_low, pair_in, pair_out, line_in, mid_ref,
    gathered, wgu, wd, hidden, whole, own_part, own_sum, send_x, recv_x, recv_z,
    w_sem, s_send, s_recv, q_send, q_recv, own_sem, k_send, k_recv, v_send, v_recv,
    p_send, p_recv, t_send, t_recv, c_send, c_recv, y_send, y_recv,
    g_send, g_recv, x_send, x_recv, z_send, z_recv,
):
    rows, width = states_ref.shape
    heads = query.shape[0]
    node_rows = keys_hbm.shape[1]
    slots = slot_node.shape[0]
    me = lax.axis_index("blk")
    head = lax.axis_index("head")
    mine, rest = me // spread_count, me % spread_count
    scale = HD ** (-0.5)

    loads = [pltpu.make_async_copy(wqkv_hbm.at[c], wqkv.at[c], w_sem.at[c]) for c in range(3)]
    loads.append(pltpu.make_async_copy(wout_hbm, wout, w_sem.at[3]))
    late = [
        pltpu.make_async_copy(wgu_hbm.at[0], wgu.at[0], w_sem.at[4]),
        pltpu.make_async_copy(wgu_hbm.at[1], wgu.at[1], w_sem.at[5]),
        pltpu.make_async_copy(wd_hbm, wd, w_sem.at[6]),
    ]
    for load in loads:
        load.start()

    def holder(index):
        return index * spread_count + rest

    peers = [{"head": (head + j) % 4} for j in range(1, 4)]
    peers += [{"blk": holder((mine + j) % heads)} for j in range(1, heads)]
    peers += [{"blk": mine * spread_count + (rest + j) % spread_count} for j in range(1, spread_count)]
    lines = slots // 2
    if spread_count != 2:
        peers += [{"blk": me // 2 * 2 + 1 - me % 2}]
        peers += [{"blk": (me // 2 + j) % lines * 2 + me % 2} for j in range(1, lines)]
    meet(peers)

    def column(index):
        return pl.ds(pl.multiple_of(index * HD, HD), HD)

    def place(buffer, index, member):
        return buffer.at[member, pl.ds(pl.multiple_of(index * node_rows, node_rows), node_rows)]

    def cache_out(target):
        return (
            remote(keys_hbm.at[0, :, column(target)], place(keys_in, mine, rest), k_send.at[0, target], k_recv.at[mine, rest], blk=holder(target)),
            remote(values_hbm.at[0, :, column(target)], place(values_in, mine, rest), v_send.at[0, target], v_recv.at[mine, rest], blk=holder(target)),
        )

    def cache_wait(source, member):
        far = holder((mine + 1) % heads)
        spot, spot_too = place(keys_in, source, member), place(values_in, source, member)
        remote(spot, spot, k_send.at[0, 0], k_recv.at[source, member], blk=far).wait_recv()
        remote(spot_too, spot_too, v_send.at[0, 0], v_recv.at[source, member], blk=far).wait_recv()

    def cache_on(source, j, own):
        target = mine * spread_count + (rest + j) % spread_count
        spot, spot_too = place(keys_in, source, rest), place(values_in, source, rest)
        from_keys = keys_hbm.at[0, :, column(mine)] if own else spot
        from_values = values_hbm.at[0, :, column(mine)] if own else spot_too
        return (
            remote(from_keys, spot, k_send.at[j, source], k_recv.at[source, rest], blk=target),
            remote(from_values, spot_too, v_send.at[j, source], v_recv.at[source, rest], blk=target),
        )

    for j in range(1, heads):
        for copy in cache_out((mine + j) % heads):
            copy.start()
    for j in range(1, spread_count):
        for copy in cache_on(mine, j, True):
            copy.start()
    own_copies = [
        pltpu.make_async_copy(keys_hbm.at[0, :, column(mine)], place(keys_in, mine, rest), own_sem.at[0]),
        pltpu.make_async_copy(values_hbm.at[0, :, column(mine)], place(values_in, mine, rest), own_sem.at[1]),
    ]
    for copy in own_copies:
        copy.start()

    def pass_on(step):
        source = by_distance(mine, heads, step)
        cache_wait(source, rest)
        for j in range(1, spread_count):
            for copy in cache_on(source, j, False):
                copy.start()

    leaves, middles, nodes = leaf_node.shape[1], node_parent.shape[0], node_length.shape[0]

    def upright(lines_of):
        filled = HD - len(lines_of)
        return jnp.transpose(jnp.concatenate(lines_of + [jnp.zeros((filled, rows), F32)], axis=0))

    def seen_by(group):
        segment = segment_ref[pl.ds(group, 1), :]
        middle, root = jnp.zeros_like(segment), jnp.zeros_like(segment)
        for leaf in range(leaves):
            middle = jnp.where(segment == leaf, leaf_node[group, leaf], middle)
        for index in range(middles):
            root = jnp.where(middle == nodes - middles + index, node_parent[index], root)
        middle_rows, root_rows = jnp.zeros_like(segment), jnp.zeros_like(segment)
        for node in range(nodes):
            middle_rows = jnp.where(middle == node, node_length[node], middle_rows)
            root_rows = jnp.where(root == node, node_length[node], root_rows)
        return segment, middle, root, middle_rows, root_rows

    for g in range(heads):
        _, middle, root, middle_rows, root_rows = seen_by(holder(g))
        lines_of = []
        for j in range(spread_count):
            for index in range(heads):
                node = slot_node[index * spread_count + (rest + j) % spread_count]
                row = jnp.where(middle == node, middle_rows, jnp.where(root == node, root_rows, 0))
                lines_of.append(row.astype(F32))
        limits[g] = upright(lines_of)
    segment, _, _, middle_rows, root_rows = seen_by(me)
    first = jnp.zeros_like(segment)
    start = jnp.zeros((1, 1), F32)
    first = jnp.zeros(segment.shape, F32)
    for leaf in range(leaves):
        inside = (segment == leaf).astype(F32)
        first = first + inside * start
        start = start + jnp.sum(inside, axis=-1, keepdims=True)
    token = lax.broadcasted_iota(jnp.int32, (1, rows), 1)
    position = (middle_rows + root_rows + token).astype(F32) - first
    own_info[...] = upright([first, position])

    tile = 2 * HD
    here = heads * HD

    def product(c):
        loads[c].wait()

        @pl.loop(0, here // tile)
        def _(t):
            at = pl.ds(pl.multiple_of(t * tile, tile), tile)
            raw[c, :, at] = jnp.dot(states_ref[...], wqkv[c, :, at], preferred_element_type=F32)

    lane = lax.broadcasted_iota(jnp.int32, (rows, HD), 1)
    product(0)
    product(1)
    query_sum = jnp.sum(raw[0] * raw[0], axis=-1, keepdims=True)
    key_sum = jnp.sum(raw[1] * raw[1], axis=-1, keepdims=True)
    packed = jnp.where(lane == 0, query_sum, jnp.where(lane == 1, key_sum, 0.0))
    squares[head] = jnp.transpose(packed)[0:8]

    def squares_to(target):
        return remote(squares.at[head], squares.at[head], s_send.at[target], s_recv.at[head], head=target)

    for j in range(1, 4):
        squares_to((head + j) % 4).start()
    pass_on(1)
    product(2)
    for load in late:
        load.start()
    value[...] = raw[2].astype(BF16)
    pass_on(2)
    angles = own_info[:, 1:2] * frequency_ref[...]
    cos_ref[...] = jnp.cos(angles)
    sines = jnp.sin(angles)
    sin_ref[...] = jnp.where(lane < HD // 2, -sines, sines)
    total = squares[head]
    for j in range(1, 4):
        source = (head + j) % 4
        remote(squares.at[source], squares.at[source], s_send.at[source], s_recv.at[source], head=source).wait_recv()
        total = total + squares[source]
    spread = jnp.transpose(jnp.concatenate([total] * (HD // 8), axis=0))
    scales = lax.rsqrt(spread / width + EPS)
    query_scale, key_scale = scales[:, 0:1], scales[:, 1:2]

    def turned(c, h, by):
        at = slice(h * HD, (h + 1) * HD)
        normed = raw[c, :, at] * by * gain_ref[c : c + 1, at]
        swapped = pltpu.roll(normed, HD // 2, 1)
        return (normed * cos_ref[...] + swapped * sin_ref[...]).astype(BF16)

    for h in range(heads):
        query[h] = turned(0, h, query_scale)

    def query_to(target):
        return remote(query.at[target], query_in.at[mine], q_send.at[target], q_recv.at[mine], blk=holder(target))

    for j in range(1, heads):
        query_to((mine + j) % heads).start()
    query_in[mine] = query[mine]
    for h in range(heads):
        key[h] = turned(1, h, key_scale)
    for step in range(3, heads):
        pass_on(step)

    row_at = lax.broadcasted_iota(jnp.int32, (rows, rows), 0)
    key_at = lax.broadcasted_iota(jnp.int32, (rows, rows), 1)
    see_leaf = (key_at.astype(F32) >= own_info[:, 0:1]) & (key_at <= row_at)
    over = (((1,), (1,)), ((), ()))
    for h in range(heads):
        scores = lax.dot_general(query[h], key[h], over, preferred_element_type=F32) * scale
        scores = jnp.where(see_leaf, scores, NEG)
        top = jnp.max(scores, axis=-1, keepdims=True)
        weights = jnp.exp(scores - top)
        leaf_peak[h] = jnp.broadcast_to(top, (rows, HD))
        leaf_norm[h] = jnp.broadcast_to(jnp.sum(weights, axis=-1, keepdims=True), (rows, HD))
        leaf_acc[h] = jnp.dot(weights.astype(BF16), value[:, h * HD : (h + 1) * HD], preferred_element_type=F32)

    for j in range(1, heads):
        source = (mine + j) % heads
        remote(query.at[0], query_in.at[source], q_send.at[0], q_recv.at[source], blk=holder(source)).wait_recv()
    key_row = lax.broadcasted_iota(jnp.int32, (rows, node_rows), 1).astype(F32)

    def part_to(target):
        return (
            remote(part_out.at[target], part_in.at[mine], p_send.at[target], p_recv.at[mine], blk=holder(target)),
            remote(stat_out.at[target], stat_in.at[mine], t_send.at[target], t_recv.at[mine], blk=holder(target)),
        )

    for copy in own_copies:
        copy.wait()
    for j in range(spread_count):
        member = (rest + j) % spread_count
        if j > 0:
            for step in range(heads):
                cache_wait(by_distance(mine, heads, step), member)

        @pl.loop(0, heads)
        def _(turn):
            g = (mine + 1 + turn) % heads
            scores = lax.dot_general(query_in[g], keys_in[member], over, preferred_element_type=F32) * scale
            limit = limits[g]
            masked = [
                jnp.where(
                    key_row < limit[:, j * heads + index : j * heads + index + 1],
                    scores[:, index * node_rows : (index + 1) * node_rows],
                    NEG,
                )
                for index in range(heads)
            ]
            highest = functools.reduce(jnp.maximum, masked)
            top = jnp.max(highest, axis=-1, keepdims=True)
            if j > 0:
                top = jnp.maximum(top, peak[g][:, 0:1])
            weights = [jnp.exp(part - top) for part in masked]
            total = jnp.sum(functools.reduce(jnp.add, weights), axis=-1, keepdims=True)
            summed = jnp.dot(
                jnp.concatenate([part.astype(BF16) for part in weights], axis=-1),
                values_in[member],
                preferred_element_type=F32,
            )
            if j > 0:
                shrink = jnp.exp(peak[g][:, 0:1] - top)
                total = total + norm[g][:, 0:1] * shrink
                summed = summed + acc[g] * shrink
            if j < spread_count - 1:
                peak[g] = jnp.broadcast_to(top, (rows, HD))
                norm[g] = jnp.broadcast_to(total, (rows, HD))
                acc[g] = summed
            else:
                part_out[g] = (summed / total).astype(BF16)
                stats = jnp.where(lane == 0, top, jnp.where(lane == 1, total, 0.0))
                stat_out[g] = jnp.transpose(stats)[0:8]

                @pl.when(turn < heads - 1)
                def _():
                    for copy in part_to(g):
                        copy.start()

    part_in[mine] = part_out[mine]
    stat_in[mine] = stat_out[mine]
    for j in range(1, heads):
        source = (mine + j) % heads
        remote(part_out.at[0], part_in.at[source], p_send.at[0], p_recv.at[source], blk=holder(source)).wait_recv()
        remote(stat_out.at[0], stat_in.at[source], t_send.at[0], t_recv.at[source], blk=holder(source)).wait_recv()
    for h in range(heads):
        stats = jnp.transpose(jnp.concatenate([stat_in[h]] * (HD // 8), axis=0))
        other_peak, other_norm = stats[:, 0:1], stats[:, 1:2]
        top = jnp.maximum(leaf_peak[h], other_peak)
        own_scale = jnp.exp(leaf_peak[h] - top)
        other_scale = jnp.exp(other_peak - top) * other_norm
        summed = leaf_acc[h] * own_scale + part_in[h].astype(F32) * other_scale
        attended[:, h * HD : (h + 1) * HD] = (
            summed / (leaf_norm[h] * own_scale + other_scale)
        ).astype(BF16)

    loads[3].wait()
    y, core = head // 2, head % 2
    own_rows = out_ref.shape[0]
    sibling, across = y * 2 + 1 - core, (1 - y) * 2 + core
    tiles = c_send.shape[1]
    wide = width // tiles

    def rows_of(index):
        return pl.ds(pl.multiple_of(index * own_rows, own_rows), own_rows)

    def cols_of(t):
        return pl.ds(t * wide, wide)

    def to_pair(half, t):
        return remote(
            proj_low.at[rows_of(half * 2 + 1 - core), cols_of(t)],
            pair_in.at[half, :, cols_of(t)],
            c_send.at[half, t], c_recv.at[half, t], head=sibling,
        )

    def to_line(t):
        return remote(pair_out.at[:, cols_of(t)], line_in.at[:, cols_of(t)], y_send.at[t], y_recv.at[t], head=across)

    def on_line(t):
        to_pair(1 - y, t).wait_recv()
        pair_out[:, cols_of(t)] = (
            proj[rows_of(across), cols_of(t)] + pair_in[1 - y, :, cols_of(t)].astype(F32)
        ).astype(BF16)
        to_line(t).start()

    for t in range(tiles):
        tiled = jnp.dot(attended[...], wout[:, cols_of(t)], preferred_element_type=F32)
        proj[:, cols_of(t)] = tiled
        proj_low[:, cols_of(t)] = tiled.astype(BF16)
        to_pair(1 - y, t).start()
        to_pair(y, t).start()
        if t > 0:
            on_line(t - 1)
    on_line(tiles - 1)
    for t in range(tiles):
        to_pair(y, t).wait_recv()
        to_line(t).wait_recv()
    total = proj[rows_of(head), :] + pair_in[y].astype(F32) + line_in[...].astype(F32)
    shrink = lax.rsqrt(jnp.mean(total * total, axis=-1, keepdims=True) + EPS)
    own = states_ref[rows_of(head), :].astype(F32)
    mid_ref[...] = (own + total * shrink * post_ref[0:1, :]).astype(BF16)

    mlp_part(
        lines, late,
        mid_ref, post_ref, out_ref,
        gathered, wgu, wd, hidden, whole, own_part, own_sum, send_x, recv_x, recv_z,
        g_send, g_recv, x_send, x_recv, z_send, z_recv,
    )

    for t in range(tiles):
        to_line(t).wait_send()
        for half in range(2):
            to_pair(half, t).wait_send()
    for j in range(1, 4):
        squares_to((head + j) % 4).wait_send()
    for j in range(1, heads):
        target = (mine + j) % heads
        query_to(target).wait_send()
        for copy in cache_out(target) + part_to(target):
            copy.wait_send()
    for source in range(heads):
        for j in range(1, spread_count):
            for copy in cache_on(source, j, False):
                copy.wait_send()


def on_device(
    states_in,
    w_qkv,
    qk_gain,
    w_out,
    post_gain,
    w_gate_up,
    w_down,
    cache_keys,
    cache_values,
    slot_node,
    node_length,
    node_parent,
    leaf_segment,
    leaf_node,
):
    rows, width = states_in.shape
    here = w_qkv.shape[2]
    heads = here // HD
    node_rows = cache_keys.shape[1]
    own_rows = rows // 4
    units = w_down.shape[0]
    slots = slot_node.shape[0]
    spread_count = slots // heads
    lines = slots // 2
    tiles = 4
    vmem = pl.BlockSpec(memory_space=pltpu.VMEM)
    smem = pl.BlockSpec(memory_space=pltpu.SMEM)
    hbm = pl.BlockSpec(memory_space=pl.ANY)
    dma = pltpu.SemaphoreType.DMA
    half = HD // 2
    frequency = THETA ** (-2.0 * jnp.arange(half, dtype=F32) / HD)

    def per_head(kind):
        return pltpu.VMEM((heads, rows, HD), kind)

    cached = pltpu.VMEM((spread_count, heads * node_rows, HD), BF16)
    part = pltpu.VMEM((lines, own_rows, width), BF16)
    return pl.pallas_call(
        functools.partial(layer_kernel, spread_count),
        out_shape=jax.ShapeDtypeStruct((own_rows, width), BF16),
        in_specs=[vmem, hbm, vmem, hbm, vmem, hbm, hbm, hbm, hbm, smem, smem, smem, vmem, smem, vmem],
        out_specs=vmem,
        scratch_shapes=[
            pltpu.VMEM(w_qkv.shape, BF16),
            pltpu.VMEM(w_out.shape, BF16),
            pltpu.VMEM((3, rows, here), F32),
            per_head(BF16),
            per_head(BF16),
            pltpu.VMEM((rows, here), BF16),
            pltpu.VMEM((4, 8, rows), F32),
            per_head(BF16),
            cached,
            cached,
            pltpu.VMEM((rows, HD), F32),
            pltpu.VMEM((rows, HD), F32),
            per_head(F32),
            pltpu.VMEM((rows, HD), F32),
            per_head(F32), per_head(F32), per_head(F32),
            per_head(F32), per_head(F32), per_head(F32),
            per_head(BF16), per_head(BF16),
            pltpu.VMEM((heads, 8, rows), F32),
            pltpu.VMEM((heads, 8, rows), F32),
            pltpu.VMEM((rows, here), BF16),
            pltpu.VMEM((rows, width), F32),
            pltpu.VMEM((rows, width), BF16),
            pltpu.VMEM((2, own_rows, width), BF16),
            pltpu.VMEM((own_rows, width), BF16),
            pltpu.VMEM((own_rows, width), BF16),
            pltpu.VMEM((own_rows, width), BF16),
            pltpu.VMEM((slots * own_rows, width), BF16),
            pltpu.VMEM(w_gate_up.shape, BF16),
            pltpu.VMEM(w_down.shape, BF16),
            pltpu.VMEM((2 * own_rows, units), BF16),
            pltpu.VMEM((2 * own_rows, width), F32),
            pltpu.VMEM((2, own_rows, width), F32),
            pltpu.VMEM((own_rows, width), F32),
            part, part, part,
            dma((7,)),
            dma((4,)), dma((4,)),
            dma((heads,)), dma((heads,)),
            dma((2,)),
            dma((spread_count, heads)), dma((heads, spread_count)),
            dma((spread_count, heads)), dma((heads, spread_count)),
            dma((heads,)), dma((heads,)),
            dma((heads,)), dma((heads,)),
            dma((2, tiles)), dma((2, tiles)),
            dma((tiles,)), dma((tiles,)),
            dma((3, slots)),
            dma((slots,)),
            dma((lines,)), dma((lines,)),
            dma((lines,)), dma((lines,)),
        ],
        compiler_params=pltpu.CompilerParams(
            collective_id=1, has_side_effects=True, vmem_limit_bytes=62 * 2**20
        ),
    )(
        states_in, w_qkv, qk_gain, w_out, post_gain, w_gate_up, w_down, cache_keys, cache_values,
        slot_node, node_length, node_parent, leaf_segment, leaf_node,
        jnp.concatenate([frequency, frequency])[None, :],
    )


def solution(mesh):
    placed = (
        P("blk", None),
        P(None, None, "head"),
        P(None, "head"),
        P("head", None),
        P(),
        P(None, None, "blk"),
        P("blk", None),
        P("blk", None, "head"),
        P("blk", None, "head"),
        P(),
        P(),
        P(),
        P(),
        P(),
    )
    return jax.shard_map(
        on_device, mesh=mesh, in_specs=placed, out_specs=P(("blk", "head"), None), check_vma=False
    )
```

time: 142 us -> 115 us (0.81)
  the two profiles are of different devices: /device:TPU:0 before, /device:TPU:24 now
where the time goes in v3:
time: 115 us
  Pallas kernels  112 us (97%)
  local copies, waits for them, and re-layouts  1.67 us (1%)
    pallas_call x1, Pallas kernels, on_device(): pl.pallas_call(functools.partial(layer_kernel, spread_count), out_shape=j...  112 us

profile of v3, /device:TPU:24, one launch (start us, length us, event | category | flops | bytes accessed | tf_op | source)
XLA Modules:
  0.0 114.7 jit_solution(9344323402741749759)
XLA Ops:
  0.0 0.6 maximum_bitcast_fusion.frequency_ref
  0.6 112.4 %shard_map.136 = bf16[64,2048]{1,0:T(8,128)(2,1)} custom-call(bf16[256,2048]{1,0:T(8,128)(2,1)} %states_ref.1, bf16[3,2048,512]{2,1,0:T(8,128)(2,1)} %wqkv_hbm.1, f32[2,512]{1,0:T(2,128)} %gain_ref.1, bf16[512,2048]{1,0:T(8,128)(2,1)} %wout_hbm.1, f32[2,2048]{1,0:T(2,128)} %post_ref.1, bf16[2,2048,1024]{2,1,0:T(8,128)(2,1)} %wgu_hbm.1, ...), custom_call_target="tpu_custom_call" | custom-call | tf_op jit(solution)/shard_map/pallas_call | solution.py:551
  113.0 1.7 %copy.16 = bf16[64,2048]{1,0:T(8,128)(2,1)} copy(bf16[64,2048]{1,0:T(8,128)(2,1)} %shard_map.136) | data formatting | bytes 524288
  (1 shorter events, 0.0 us)

commit v4 on v3

--- a/solution.py
+++ b/solution.py
@@ -38,7 +38,7 @@
     barrier = pltpu.get_barrier_semaphore()
     for peer in peers:
         pl.semaphore_signal(barrier, inc=1, device_id=peer, device_id_type=MESH)
-    pl.semaphore_wait(barrier, len(peers))
+    return lambda: pl.semaphore_wait(barrier, len(peers))
 
 
 def mlp_part(
@@ -76,25 +76,40 @@
     gathered[pl.ds(pl.multiple_of(me * rows, rows), rows), :] = mid_ref[...]
     spread(z, False)
 
-    def to_x(origin):
-        return remote(send_x.at[origin], recv_x.at[origin], x_send.at[origin], x_recv.at[origin], blk=other)
-
-    def to_z(origin):
-        return remote(send_x.at[origin], recv_z.at[z], z_send.at[origin], z_recv.at[z], blk=origin * 2 + x)
+    tiles = x_send.shape[1]
+    wide = width // tiles
+
+    def cols_of(t):
+        return pl.ds(pl.multiple_of(t * wide, wide), wide)
+
+    def to_x(origin, t):
+        return remote(
+            send_x.at[origin, :, cols_of(t)], recv_x.at[origin, :, cols_of(t)],
+            x_send.at[origin, t], x_recv.at[origin, t], blk=other,
+        )
+
+    def to_z(origin, t):
+        return remote(
+            send_x.at[origin, :, cols_of(t)], recv_z.at[z, :, cols_of(t)],
+            z_send.at[origin, t], z_recv.at[z, t], blk=origin * 2 + x,
+        )
 
     def reduce_x(step):
         origin = by_distance(z, lines, step)
-        to_x(origin).wait_recv()
-        summed = own_part[step % 2] + recv_x[origin].astype(F32)
-        to_x(origin).wait_send()
-        if step == 0:
-            own_sum[...] = summed
-        else:
-            send_x[origin] = summed.astype(BF16)
-            to_z(origin).start()
+
+        @pl.loop(0, tiles)
+        def _(t):
+            at = cols_of(t)
+            to_x(origin, t).wait_recv()
+            summed = own_part[step % 2, :, at] + recv_x[origin, :, at].astype(F32)
+            to_x(origin, t).wait_send()
+            if step == 0:
+                own_sum[:, at] = summed
+            else:
+                send_x[origin, :, at] = summed.astype(BF16)
+                to_z(origin, t).start()
 
     tile = min(256, units)
-    wide = min(512, width)
     for step in range(lines):
         origin = by_distance(z, lines, step)
         if step + 1 < lines:
@@ -116,14 +131,16 @@
         if step == 0:
             loads[2].wait()
 
-        @pl.loop(0, width // wide)
+        @pl.loop(0, tiles)
         def _(t):
-            at = pl.ds(pl.multiple_of(t * wide, wide), wide)
+            at = cols_of(t)
             whole[:, at] = jnp.dot(hidden[...], wd[:, at], preferred_element_type=F32)
-
-        own_part[step % 2] = whole[pl.ds(pl.multiple_of(x * rows, rows), rows), :]
-        send_x[origin] = whole[pl.ds(pl.multiple_of((1 - x) * rows, rows), rows), :].astype(BF16)
-        to_x(origin).start()
+            own_part[step % 2, :, at] = whole[pl.ds(pl.multiple_of(x * rows, rows), rows), at]
+            send_x[origin, :, at] = whole[
+                pl.ds(pl.multiple_of((1 - x) * rows, rows), rows), at
+            ].astype(BF16)
+            to_x(origin, t).start()
+
         if step > 0:
             reduce_x(step - 1)
     reduce_x(lines - 1)
@@ -131,7 +148,9 @@
     total = own_sum[...]
     for j in range(1, lines):
         source = (z + j) % lines
-        remote(send_x.at[0], recv_z.at[source], z_send.at[0], z_recv.at[source], blk=other).wait_recv()
+        for t in range(tiles):
+            spot = recv_z.at[source, :, cols_of(t)]
+            remote(spot, spot, z_send.at[0, t], z_recv.at[source, t], blk=other).wait_recv()
         total = total + recv_z[source].astype(F32)
     scale = lax.rsqrt(jnp.mean(total * total, axis=-1, keepdims=True) + EPS)
     out_ref[...] = (mid_ref[...].astype(F32) + total * scale * gain_ref[1:2, :]).astype(BF16)
@@ -150,7 +169,8 @@
 
         @pl.when(origin != z)
         def _():
-            to_z(origin).wait_send()
+            for t in range(tiles):
+                to_z(origin, t).wait_send()
 
 
 def layer_kernel(
@@ -195,7 +215,7 @@
     if spread_count != 2:
         peers += [{"blk": me // 2 * 2 + 1 - me % 2}]
         peers += [{"blk": (me // 2 + j) % lines * 2 + me % 2} for j in range(1, lines)]
-    meet(peers)
+    all_here = meet(peers)
 
     def column(index):
         return pl.ds(pl.multiple_of(index * HD, HD), HD)
@@ -225,12 +245,6 @@
             remote(from_values, spot_too, v_send.at[j, source], v_recv.at[source, rest], blk=target),
         )
 
-    for j in range(1, heads):
-        for copy in cache_out((mine + j) % heads):
-            copy.start()
-    for j in range(1, spread_count):
-        for copy in cache_on(mine, j, True):
-            copy.start()
     own_copies = [
         pltpu.make_async_copy(keys_hbm.at[0, :, column(mine)], place(keys_in, mine, rest), own_sem.at[0]),
         pltpu.make_async_copy(values_hbm.at[0, :, column(mine)], place(values_in, mine, rest), own_sem.at[1]),
@@ -274,9 +288,8 @@
                 lines_of.append(row.astype(F32))
         limits[g] = upright(lines_of)
     segment, _, _, middle_rows, root_rows = seen_by(me)
-    first = jnp.zeros_like(segment)
+    first = jnp.zeros(segment.shape, F32)
     start = jnp.zeros((1, 1), F32)
-    first = jnp.zeros(segment.shape, F32)
     for leaf in range(leaves):
         inside = (segment == leaf).astype(F32)
         first = first + inside * start
@@ -285,6 +298,14 @@
     position = (middle_rows + root_rows + token).astype(F32) - first
     own_info[...] = upright([first, position])
 
+    all_here()
+    for j in range(1, heads):
+        for copy in cache_out((mine + j) % heads):
+            copy.start()
+    for j in range(1, spread_count):
+        for copy in cache_on(mine, j, True):
+            copy.start()
+
     tile = 2 * HD
     here = heads * HD
 
@@ -309,12 +330,10 @@
 
     for j in range(1, 4):
         squares_to((head + j) % 4).start()
-    pass_on(1)
     product(2)
     for load in late:
         load.start()
     value[...] = raw[2].astype(BF16)
-    pass_on(2)
     angles = own_info[:, 1:2] * frequency_ref[...]
     cos_ref[...] = jnp.cos(angles)
     sines = jnp.sin(angles)
@@ -343,10 +362,10 @@
     for j in range(1, heads):
         query_to((mine + j) % heads).start()
     query_in[mine] = query[mine]
+    for step in range(1, heads):
+        pass_on(step)
     for h in range(heads):
         key[h] = turned(1, h, key_scale)
-    for step in range(3, heads):
-        pass_on(step)
 
     row_at = lax.broadcasted_iota(jnp.int32, (rows, rows), 0)
     key_at = lax.broadcasted_iota(jnp.int32, (rows, rows), 1)
@@ -600,8 +619,8 @@
             dma((tiles,)), dma((tiles,)),
             dma((3, slots)),
             dma((slots,)),
-            dma((lines,)), dma((lines,)),
-            dma((lines,)), dma((lines,)),
+            dma((lines, tiles)), dma((lines, tiles)),
+            dma((lines, tiles)), dma((lines, tiles)),
         ],
         compiler_params=pltpu.CompilerParams(
             collective_id=1, has_side_effects=True, vmem_limit_bytes=62 * 2**20

time: 115 us -> 112 us (0.974)
  the two profiles are of different devices: /device:TPU:24 before, /device:TPU:0 now
where the time goes in v4:
time: 112 us; the launch traced here: 110 us
  Pallas kernels  108 us (96%)
  local copies, waits for them, and re-layouts  1.67 us (1%)
    pallas_call x1, Pallas kernels, on_device(): pl.pallas_call(functools.partial(layer_kernel, spread_count), out_shape=j...  108 us

profile of v4, /device:TPU:0, one launch (start us, length us, event | category | flops | bytes accessed | tf_op | source)
XLA Modules:
  0.0 110.0 jit_solution(4190531221364116525)
XLA Ops:
  0.0 0.6 maximum_bitcast_fusion.frequency_ref
  0.6 107.7 %shard_map.136 = bf16[64,2048]{1,0:T(8,128)(2,1)} custom-call(bf16[256,2048]{1,0:T(8,128)(2,1)} %states_ref.1, bf16[3,2048,512]{2,1,0:T(8,128)(2,1)} %wqkv_hbm.1, f32[2,512]{1,0:T(2,128)} %gain_ref.1, bf16[512,2048]{1,0:T(8,128)(2,1)} %wout_hbm.1, f32[2,2048]{1,0:T(2,128)} %post_ref.1, bf16[2,2048,1024]{2,1,0:T(8,128)(2,1)} %wgu_hbm.1, ...), custom_call_target="tpu_custom_call" | custom-call | tf_op jit(solution)/shard_map/pallas_call | solution.py:570
  108.3 1.7 %copy.16 = bf16[64,2048]{1,0:T(8,128)(2,1)} copy(bf16[64,2048]{1,0:T(8,128)(2,1)} %shard_map.136) | data formatting | bytes 524288
  (1 shorter events, 0.0 us)

commit v5 on v4

--- a/solution.py
+++ b/solution.py
@@ -63,7 +63,10 @@
         index = origin * 2 + x
         if wait:
             pass_on(index, 0, other).wait_recv()
-        pass_on(index, 0, other).start()
+
+        @pl.when((origin - z) * (origin - z) != 1)
+        def _():
+            pass_on(index, 0, other).start()
 
         @pl.when((origin <= z) & (z < lines - 1))
         def _():
@@ -103,11 +106,10 @@
             to_x(origin, t).wait_recv()
             summed = own_part[step % 2, :, at] + recv_x[origin, :, at].astype(F32)
             to_x(origin, t).wait_send()
-            if step == 0:
-                own_sum[:, at] = summed
-            else:
-                send_x[origin, :, at] = summed.astype(BF16)
-                to_z(origin, t).start()
+            send_x[origin, :, at] = summed.astype(BF16)
+            to_z(origin, t).start()
+            if step == lines - 1:
+                to_x(z, t).start()
 
     tile = min(256, units)
     for step in range(lines):
@@ -116,6 +118,14 @@
             spread(by_distance(z, lines, step + 1), True)
         pass_on(origin * 2 + 1 - x, 0, other).wait_recv()
         if step == 0:
+            @pl.when(z < lines - 1)
+            def _():
+                pass_on(other, 1, me + 2).start()
+
+            @pl.when(z > 0)
+            def _():
+                pass_on(other, 2, me - 2).start()
+
             loads[0].wait()
             loads[1].wait()
         chunk = pl.ds(pl.multiple_of(origin * 2 * rows, 2 * rows), 2 * rows)
@@ -135,17 +145,24 @@
         def _(t):
             at = cols_of(t)
             whole[:, at] = jnp.dot(hidden[...], wd[:, at], preferred_element_type=F32)
-            own_part[step % 2, :, at] = whole[pl.ds(pl.multiple_of(x * rows, rows), rows), at]
+            kept = whole[pl.ds(pl.multiple_of(x * rows, rows), rows), at]
+            if step == 0:
+                own_sum[:, at] = kept
+            else:
+                own_part[step % 2, :, at] = kept
             send_x[origin, :, at] = whole[
                 pl.ds(pl.multiple_of((1 - x) * rows, rows), rows), at
             ].astype(BF16)
-            to_x(origin, t).start()
-
-        if step > 0:
+            if step > 0:
+                to_x(origin, t).start()
+
+        if step > 1:
             reduce_x(step - 1)
     reduce_x(lines - 1)
 
-    total = own_sum[...]
+    for t in range(tiles):
+        to_x(z, t).wait_recv()
+    total = own_sum[...] + recv_x[z].astype(F32)
     for j in range(1, lines):
         source = (z + j) % lines
         for t in range(tiles):
@@ -155,9 +172,23 @@
     scale = lax.rsqrt(jnp.mean(total * total, axis=-1, keepdims=True) + EPS)
     out_ref[...] = (mid_ref[...].astype(F32) + total * scale * gain_ref[1:2, :]).astype(BF16)
 
+    for t in range(tiles):
+        to_x(z, t).wait_send()
+
+    @pl.when(z < lines - 1)
+    def _():
+        pass_on(other, 1, me + 2).wait_send()
+
+    @pl.when(z > 0)
+    def _():
+        pass_on(other, 2, me - 2).wait_send()
+
     for origin in range(lines):
         index = origin * 2 + x
-        pass_on(index, 0, other).wait_send()
+
+        @pl.when((origin - z) * (origin - z) != 1)
+        def _():
+            pass_on(index, 0, other).wait_send()
 
         @pl.when((origin <= z) & (z < lines - 1))
         def _():

time: 112 us -> 107 us (0.955); the launches traced: 110 us -> 107 us
  Pallas kernels: 108 us -> 105 us
    pallas_call x1, Pallas kernels: 108 us -> 105 us  [on_device(): pl.pallas_call(functools.partial(layer_kernel, spread_count), out_shape=j...]
where the time goes in v5:
time: 107 us
  Pallas kernels  105 us (98%)
  local copies, waits for them, and re-layouts  1.67 us (2%)
    pallas_call x1, Pallas kernels, on_device(): pl.pallas_call(functools.partial(layer_kernel, spread_count), out_shape=j...  105 us

profile of v5, /device:TPU:0, one launch (start us, length us, event | category | flops | bytes accessed | tf_op | source)
XLA Modules:
  0.0 107.1 jit_solution(11474391930519757633)
XLA Ops:
  0.0 0.6 maximum_bitcast_fusion.frequency_ref
  0.6 104.8 %shard_map.136 = bf16[64,2048]{1,0:T(8,128)(2,1)} custom-call(bf16[256,2048]{1,0:T(8,128)(2,1)} %states_ref.1, bf16[3,2048,512]{2,1,0:T(8,128)(2,1)} %wqkv_hbm.1, f32[2,512]{1,0:T(2,128)} %gain_ref.1, bf16[512,2048]{1,0:T(8,128)(2,1)} %wout_hbm.1, f32[2,2048]{1,0:T(2,128)} %post_ref.1, bf16[2,2048,1024]{2,1,0:T(8,128)(2,1)} %wgu_hbm.1, ...), custom_call_target="tpu_custom_call" | custom-call | tf_op jit(solution)/shard_map/pallas_call | solution.py:601
  105.5 1.7 %copy.16 = bf16[64,2048]{1,0:T(8,128)(2,1)} copy(bf16[64,2048]{1,0:T(8,128)(2,1)} %shard_map.136) | data formatting | bytes 524288
  (1 shorter events, 0.0 us)

commit v6 on v5

--- a/solution.py
+++ b/solution.py
@@ -2,6 +2,7 @@
 
 import jax
 import jax.numpy as jnp
+import numpy as np
 from jax import lax
 from jax.experimental import pallas as pl
 from jax.experimental.pallas import tpu as pltpu
@@ -402,7 +403,7 @@
     key_at = lax.broadcasted_iota(jnp.int32, (rows, rows), 1)
     see_leaf = (key_at.astype(F32) >= own_info[:, 0:1]) & (key_at <= row_at)
     over = (((1,), (1,)), ((), ()))
-    for h in range(heads):
+    def leaf_part(h):
         scores = lax.dot_general(query[h], key[h], over, preferred_element_type=F32) * scale
         scores = jnp.where(see_leaf, scores, NEG)
         top = jnp.max(scores, axis=-1, keepdims=True)
@@ -410,6 +411,9 @@
         leaf_peak[h] = jnp.broadcast_to(top, (rows, HD))
         leaf_norm[h] = jnp.broadcast_to(jnp.sum(weights, axis=-1, keepdims=True), (rows, HD))
         leaf_acc[h] = jnp.dot(weights.astype(BF16), value[:, h * HD : (h + 1) * HD], preferred_element_type=F32)
+
+    for h in range(heads // 2):
+        leaf_part(h)
 
     for j in range(1, heads):
         source = (mine + j) % heads
@@ -474,6 +478,8 @@
 
     part_in[mine] = part_out[mine]
     stat_in[mine] = stat_out[mine]
+    for h in range(heads // 2, heads):
+        leaf_part(h)
     for j in range(1, heads):
         source = (mine + j) % heads
         remote(part_out.at[0], part_in.at[source], p_send.at[0], p_recv.at[source], blk=holder(source)).wait_recv()
@@ -591,7 +597,7 @@
     hbm = pl.BlockSpec(memory_space=pl.ANY)
     dma = pltpu.SemaphoreType.DMA
     half = HD // 2
-    frequency = THETA ** (-2.0 * jnp.arange(half, dtype=F32) / HD)
+    frequency = (THETA ** (-2.0 * np.arange(half) / HD)).astype(np.float32)
 
     def per_head(kind):
         return pltpu.VMEM((heads, rows, HD), kind)
@@ -659,7 +665,7 @@
     )(
         states_in, w_qkv, qk_gain, w_out, post_gain, w_gate_up, w_down, cache_keys, cache_values,
         slot_node, node_length, node_parent, leaf_segment, leaf_node,
-        jnp.concatenate([frequency, frequency])[None, :],
+        np.concatenate([frequency, frequency])[None, :],
     )
 
 

time: 107 us -> 107 us (level)
  no operation moved by 1% of the time
where the time goes in v6:
time: 107 us
  Pallas kernels  105 us (98%)
  local copies, waits for them, and re-layouts  1.67 us (2%)
    pallas_call x1, Pallas kernels, on_device(): pl.pallas_call(functools.partial(layer_kernel, spread_count), out_shape=j...  105 us

profile of v6, /device:TPU:0, one launch (start us, length us, event | category | flops | bytes accessed | tf_op | source)
XLA Modules:
  0.0 106.5 jit_solution(13322785650870975882)
XLA Ops:
  0.0 104.8 %shard_map.145 = bf16[64,2048]{1,0:T(8,128)(2,1)} custom-call(bf16[256,2048]{1,0:T(8,128)(2,1)} %states_ref.1, bf16[3,2048,512]{2,1,0:T(8,128)(2,1)} %wqkv_hbm.1, f32[2,512]{1,0:T(2,128)} %gain_ref.1, bf16[512,2048]{1,0:T(8,128)(2,1)} %wout_hbm.1, f32[2,2048]{1,0:T(2,128)} %post_ref.1, bf16[2,2048,1024]{2,1,0:T(8,128)(2,1)} %wgu_hbm.1, ...), custom_call_target="tpu_custom_call" | custom-call | tf_op jit(solution)/shard_map/pallas_call | solution.py:607
  104.9 1.7 %copy.17 = bf16[64,2048]{1,0:T(8,128)(2,1)} copy(bf16[64,2048]{1,0:T(8,128)(2,1)} %shard_map.145) | data formatting | bytes 524288
